TPU v7x, 128 devices: a whole 4x4x4 slice. The times are simulated.
128 devices in a mesh: leaf: 32 (over x, z, core), sub: 4 (over y).
Axes of the slice: x: 4, y: 4, z: 4, core: 2. Of those that a mesh axis runs over, the one named last changes fastest.
Arguments:
- rhs: float32 [64, 1048576], P(None, ('leaf', 'sub')), may hold values from -6 to 6
- iterate: float32 [64, 1048576], P(None, ('leaf', 'sub')), may hold values from -6 to 6
- residual: float32 [64, 1048576], P(None, ('leaf', 'sub')), may hold values from -66 to 66
- direction: float32 [64, 1048576], P(None, ('leaf', 'sub')), may hold values from -66 to 66
- points: float32 [8, 1048576], P(None, ('leaf', 'sub')), may hold values from -1.4 to 2.4
- skeletons: float32 [8, 262144], P(None, ('leaf', 'sub')), may hold values from -1.4 to 2.4
- leaf_basis: float32 [64, 1048576], P(None, ('leaf', 'sub')), may hold values from -0.75 to 0.75
- device_basis: float32 [64, 262144], P(None, ('leaf', 'sub')), may hold values from -0.375 to 0.375
- transfer: float32 [126, 64, 128], replicated, may hold values from -0.625 to 0.625
- node_coords: float32 [8, 8064], replicated, may hold values from -1.4 to 2.4
- near_list: int32 [4096, 8], P(('leaf', 'sub')), may hold values from -1 to 63, as said below
- far_list: int32 [4096, 8], P(('leaf', 'sub')), may hold values from -1 to 63, as said below
Outputs:
- new_iterate: float32 [64, 1048576], P(None, ('leaf', 'sub'))
- new_residual: float32 [64, 1048576], P(None, ('leaf', 'sub'))
- new_direction: float32 [64, 1048576], P(None, ('leaf', 'sub'))
- true_residual: float32 [64, 1048576], P(None, ('leaf', 'sub'))
Inputs may be any that keep to these rules, and one draw needn't show every extreme that they name: `near_list`: live entries of a row come first and entry 0 is the leaf itself; a row names no source twice and none that the same leaf's far_list row names; a device block holds at most 192 live entries. `far_list`: live entries of a row come first; at least half of a row is live.
All inputs are finite; a program needn't handle non-finite values.
Results may differ from a plain program's by a relative error of at most 0.0003.
Values sent between devices are 32-bit elements; how exact they have to be, the bound alone decides.
A program may use at most 256 MiB of HBM per device.

v0:
```python
import math

import jax
import jax.numpy as jnp
from jax import lax
from jax.sharding import PartitionSpec as P

noise_level = 1.0
amplitude = 0.1
length_scale = 1.0
highest = lax.Precision.HIGHEST


def from_partner(value, axis, apart):
    return lax.ppermute(value, axis, [(i, i ^ 1 << apart) for i in range(lax.axis_size(axis))])


def matern(first_pts, second_pts):
    cross = jnp.einsum("bdm,bdn->bmn", first_pts, second_pts, precision=highest)
    first_sq = jnp.sum(first_pts * first_pts, axis=1)
    second_sq = jnp.sum(second_pts * second_pts, axis=1)
    dist_sq = first_sq[:, :, None] + second_sq[:, None, :] - 2.0 * cross
    scaled = math.sqrt(3.0) / length_scale * jnp.sqrt(jnp.maximum(dist_sq, 0.0))
    return amplitude * (1.0 + scaled) * jnp.exp(-scaled)


def near_block(points_tab, vector_tab, targets, sources, weights):
    target_pts = jnp.take(points_tab, targets, axis=0)
    source_pts = jnp.take(points_tab, sources, axis=0)
    kernel = matern(source_pts, target_pts)
    source_vec = jnp.take(vector_tab, sources, axis=1)
    terms = jnp.einsum("nbq,bqp->bnp", source_vec, kernel, precision=highest)
    return terms * weights[:, None, None]


def near_terms(points_tab, vector_tab, targets, sources, weights):
    number = targets.shape[0]
    stride = math.gcd(number, 32)

    def one_block(packed):
        return near_block(points_tab, vector_tab, packed[0], packed[1], packed[2])

    shaped = (
        targets.reshape(number // stride, stride),
        sources.reshape(number // stride, stride),
        weights.reshape(number // stride, stride),
    )
    result = lax.map(one_block, shaped)
    return result.reshape(number, vector_tab.shape[0], vector_tab.shape[2])


def far_terms(skel_tab, weight_tab, far_rows):
    leaves, slots = far_rows.shape
    targets = jnp.repeat(jnp.arange(leaves, dtype=jnp.int32), slots)
    flat = far_rows.reshape(-1)
    sources = jnp.maximum(flat, 0)
    weights = (flat >= 0).astype(weight_tab.dtype)
    kernel = matern(jnp.take(skel_tab, targets, axis=0), jnp.take(skel_tab, sources, axis=0))
    terms = jnp.einsum(
        "bij,bjn->bin", kernel, jnp.take(weight_tab, sources, axis=0), precision=highest
    )
    terms = terms * weights[:, None, None]
    return terms.reshape(leaves, slots, terms.shape[1], terms.shape[2]).sum(axis=1)


def shards(
    rhs,
    iterate,
    residual,
    direction,
    points,
    skeletons,
    leaf_basis,
    device_basis,
    transfer,
    node_coords,
    near_list,
    far_list,
):
    leaves, near_slots = near_list.shape
    coord_dims = points.shape[0]
    leaf_size = points.shape[1] // leaves
    skel_rank = leaf_basis.shape[0]
    n_leaf = lax.axis_size("leaf")
    n_sub = lax.axis_size("sub")
    device_total = n_leaf * n_sub
    heights = device_total.bit_length() - 1
    leaf_bits = n_leaf.bit_length() - 1
    position = lax.axis_index("sub") * n_leaf + lax.axis_index("leaf")
    coords = node_coords.reshape(coord_dims, -1, skel_rank).transpose(1, 0, 2)
    other_points, other_skel = from_partner((points, skeletons), "leaf", 0)
    points_tab = jnp.concatenate(
        [
            points.reshape(coord_dims, leaves, leaf_size),
            other_points.reshape(coord_dims, leaves, leaf_size),
        ],
        axis=1,
    ).transpose(1, 0, 2)
    skel_tab = jnp.concatenate(
        [
            skeletons.reshape(coord_dims, leaves, skel_rank),
            other_skel.reshape(coord_dims, leaves, skel_rank),
        ],
        axis=1,
    ).transpose(1, 0, 2)
    basis3 = leaf_basis.reshape(skel_rank, leaves, leaf_size)

    def climb(dev_w, sibling):
        current = dev_w
        matrices = [None]
        coupled = [None]
        for height in range(1, heights):
            which_half = position >> height - 1 & 1
            stacked = jnp.where(
                which_half == 0,
                jnp.concatenate([current, sibling], axis=0),
                jnp.concatenate([sibling, current], axis=0),
            )
            nodes_here = device_total >> height
            offset = device_total - 2 * nodes_here
            node_here = position >> height
            matrix = lax.dynamic_index_in_dim(transfer, offset + node_here, 0, keepdims=False)
            current = jnp.dot(matrix, stacked, precision=highest)
            if height < leaf_bits:
                sibling = from_partner(current, "leaf", height)
            else:
                sibling = from_partner(current, "sub", height - leaf_bits)
            own_coords = lax.dynamic_index_in_dim(coords, offset + node_here, 0, keepdims=False)
            sib_coords = lax.dynamic_index_in_dim(
                coords, offset + (node_here ^ 1), 0, keepdims=False
            )
            kernel = matern(own_coords[None], sib_coords[None])[0]
            coupled.append(jnp.dot(kernel, sibling, precision=highest))
            matrices.append(matrix)
        downward = coupled[heights - 1]
        for height in range(heights - 1, 0, -1):
            which_half = position >> height - 1 & 1
            portion = lax.dynamic_slice_in_dim(
                matrices[height], which_half * skel_rank, skel_rank, 1
            )
            downward = jnp.dot(portion.T, downward, precision=highest)
            if height > 1:
                downward = downward + coupled[height - 1]
        return downward

    def operator(vector):
        columns = vector.shape[0]
        vec3 = vector.reshape(columns, leaves, leaf_size)
        leaf_w = jnp.einsum("rlp,nlp->lrn", basis3, vec3, precision=highest)
        dev_w = jnp.dot(
            device_basis, leaf_w.reshape(leaves * skel_rank, columns), precision=highest
        )
        other_vec, other_w, other_dev = from_partner((vec3, leaf_w, dev_w), "leaf", 0)
        bottom = climb(dev_w, other_dev)
        vector_tab = jnp.concatenate([vec3, other_vec], axis=1)
        weight_tab = jnp.concatenate([leaf_w, other_w], axis=0)
        flat = near_list.reshape(-1)
        targets = jnp.repeat(jnp.arange(leaves, dtype=jnp.int32), near_slots)
        terms = near_terms(
            points_tab, vector_tab, targets, jnp.maximum(flat, 0), (flat >= 0).astype(jnp.float32)
        )
        near_part = (
            terms.reshape(leaves, near_slots, columns, leaf_size).sum(axis=1).transpose(1, 0, 2)
        )
        z_leaf = jnp.dot(device_basis.T, bottom, precision=highest).reshape(
            leaves, skel_rank, columns
        )
        z_leaf = z_leaf + far_terms(skel_tab, weight_tab, far_list)
        far_part = jnp.einsum("rlp,lrn->nlp", basis3, z_leaf, precision=highest)
        return (noise_level * vec3 + near_part + far_part).reshape(columns, leaves * leaf_size)

    norm_old = lax.psum(jnp.sum(residual * residual, axis=1), ("leaf", "sub"))
    image = operator(direction)
    curvature = lax.psum(jnp.sum(direction * image, axis=1), ("leaf", "sub"))
    alpha = norm_old / curvature
    new_iterate = iterate + alpha[:, None] * direction
    new_residual = residual - alpha[:, None] * image
    norm_new = lax.psum(jnp.sum(new_residual * new_residual, axis=1), ("leaf", "sub"))
    new_direction = new_residual + (norm_new / norm_old)[:, None] * direction
    true_residual = rhs - operator(new_iterate)
    return (new_iterate, new_residual, new_direction, true_residual)


def solution(mesh):
    in_specs = (
        P(None, ("leaf", "sub")),
        P(None, ("leaf", "sub")),
        P(None, ("leaf", "sub")),
        P(None, ("leaf", "sub")),
        P(None, ("leaf", "sub")),
        P(None, ("leaf", "sub")),
        P(None, ("leaf", "sub")),
        P(None, ("leaf", "sub")),
        P(),
        P(),
        P(("leaf", "sub"), None),
        P(("leaf", "sub"), None),
    )
    out_specs = (
        P(None, ("leaf", "sub")),
        P(None, ("leaf", "sub")),
        P(None, ("leaf", "sub")),
        P(None, ("leaf", "sub")),
    )
    return jax.shard_map(shards, mesh=mesh, in_specs=in_specs, out_specs=out_specs, check_vma=False)
```

profile of v0, /device:TPU:0, one launch (start us, length us, event | category | flops | bytes accessed | tf_op | source)
XLA Modules:
  0.0 843.8 jit_solution(103374107469231358)
XLA Ops:
  50.8 22.0 %exponential_multiply_fusion = f32[256,64,64]{2,1,0:T(8,128)} fusion(f32[256,64]{1,0:T(8,128)S(1)} %multiply_reduce_fusion.7, f32[256,64]{1,0:T(8,128)S(1)} %multiply_reduce_fusion.8, f32[256,8,64]{2,1,0:T(8,128)S(1)} %gather_fusion.7, f32[256,8,64]{2,1,0:T(8,128)} %gather_fusion.6, pred[256]{0:T(512)(128)(4,1)} %compare_and_fusion.4, ...), kind=kOutput, calls=%fused_computation.118 | convolution fusion | flops 110362624 | bytes 5374464 | tf_op jit(solution)/shard_map/bdm,bdn->bmn/dot_general | solution.py:19
  90.2 24.3 %bitcast_reduce_fusion.1 = f32[32,64,64]{2,1,0:T(8,128)} fusion(f32[256]{0:T(256)S(1)} %reshape.510, f32[256,64,64]{2,1,0:T(8,128)} %exponential_multiply_fusion, f32[256,64,64]{2,1,0:T(8,128)} %gather_fusion.8, pred[256]{0:T(512)(128)(4,1)S(1)} %copy-done.27), kind=kOutput, calls=%fused_computation.113 | convolution fusion | flops 808321024 | bytes 8914176 | tf_op jit(solution)/shard_map/bij,bjn->bin/dot_general | solution.py:59
  129.3 224.7 %while.20 = (s32[]{:T(128)}, f32[8,32,64,256]{3,2,1,0:T(8,128)}, s32[8,32]{1,0:T(8,128)S(1)}, f32[64,64,256]{2,0,1:T(8,128)}, f32[64,8,256]{2,1,0:T(8,128)S(1)},...) while((s32[]{:T(128)}, f32[8,32,64,256]{3,2,1,0:T(8,128)}, s32[8,32]{1,0:T(8,128)S(1)}, ...), condition=%wide.region_5.8_spmd, body=%wide.region_2.7_spmd.sunk | while | flops 1832372608 | bytes 27404604 | solution.py:48
  143.8 13.7 %bitcast_dynamic-update-slice_fusion.4 = f32[8,32,64,256]{3,2,1,0:T(8,128)} fusion(f32[8,32,64,256]{3,2,1,0:T(8,128)} %get-tuple-element.347, s32[]{:T(128)} %get-tuple-element.346, f32[32,256,256]{2,1,0:T(8,128)} %fusion.413, f32[32,256]{1,0:T(8,128)S(1)} %multiply_reduce_fusion.25, f32[32,256]{1,0:T(8,128)S(1)} %multiply_reduce_fusion.26, ...), kind=kOutput, calls=%fused_computation.29.clone.1 | convolution fusion | flops 1630535680 | bytes 12649120 | tf_op jit(solution)/shard_map/while/body/eval_jaxpr/nbq,bqp->bnp/dot_general | solution.py:32
  171.9 13.6 %bitcast_dynamic-update-slice_fusion.4 = f32[8,32,64,256]{3,2,1,0:T(8,128)} fusion(f32[8,32,64,256]{3,2,1,0:T(8,128)} %get-tuple-element.347, s32[]{:T(128)} %get-tuple-element.346, f32[32,256,256]{2,1,0:T(8,128)} %fusion.413, f32[32,256]{1,0:T(8,128)S(1)} %multiply_reduce_fusion.25, f32[32,256]{1,0:T(8,128)S(1)} %multiply_reduce_fusion.26, ...), kind=kOutput, calls=%fused_computation.29.clone.1 | convolution fusion | flops 1630535680 | bytes 12649120 | tf_op jit(solution)/shard_map/while/body/eval_jaxpr/nbq,bqp->bnp/dot_general | solution.py:32
  199.9 13.6 %bitcast_dynamic-update-slice_fusion.4 = f32[8,32,64,256]{3,2,1,0:T(8,128)} fusion(f32[8,32,64,256]{3,2,1,0:T(8,128)} %get-tuple-element.347, s32[]{:T(128)} %get-tuple-element.346, f32[32,256,256]{2,1,0:T(8,128)} %fusion.413, f32[32,256]{1,0:T(8,128)S(1)} %multiply_reduce_fusion.25, f32[32,256]{1,0:T(8,128)S(1)} %multiply_reduce_fusion.26, ...), kind=kOutput, calls=%fused_computation.29.clone.1 | convolution fusion | flops 1630535680 | bytes 12649120 | tf_op jit(solution)/shard_map/while/body/eval_jaxpr/nbq,bqp->bnp/dot_general | solution.py:32
  227.9 13.6 %bitcast_dynamic-update-slice_fusion.4 = f32[8,32,64,256]{3,2,1,0:T(8,128)} fusion(f32[8,32,64,256]{3,2,1,0:T(8,128)} %get-tuple-element.347, s32[]{:T(128)} %get-tuple-element.346, f32[32,256,256]{2,1,0:T(8,128)} %fusion.413, f32[32,256]{1,0:T(8,128)S(1)} %multiply_reduce_fusion.25, f32[32,256]{1,0:T(8,128)S(1)} %multiply_reduce_fusion.26, ...), kind=kOutput, calls=%fused_computation.29.clone.1 | convolution fusion | flops 1630535680 | bytes 12649120 | tf_op jit(solution)/shard_map/while/body/eval_jaxpr/nbq,bqp->bnp/dot_general | solution.py:32
  256.0 13.6 %bitcast_dynamic-update-slice_fusion.4 = f32[8,32,64,256]{3,2,1,0:T(8,128)} fusion(f32[8,32,64,256]{3,2,1,0:T(8,128)} %get-tuple-element.347, s32[]{:T(128)} %get-tuple-element.346, f32[32,256,256]{2,1,0:T(8,128)} %fusion.413, f32[32,256]{1,0:T(8,128)S(1)} %multiply_reduce_fusion.25, f32[32,256]{1,0:T(8,128)S(1)} %multiply_reduce_fusion.26, ...), kind=kOutput, calls=%fused_computation.29.clone.1 | convolution fusion | flops 1630535680 | bytes 12649120 | tf_op jit(solution)/shard_map/while/body/eval_jaxpr/nbq,bqp->bnp/dot_general | solution.py:32
  284.0 13.6 %bitcast_dynamic-update-slice_fusion.4 = f32[8,32,64,256]{3,2,1,0:T(8,128)} fusion(f32[8,32,64,256]{3,2,1,0:T(8,128)} %get-tuple-element.347, s32[]{:T(128)} %get-tuple-element.346, f32[32,256,256]{2,1,0:T(8,128)} %fusion.413, f32[32,256]{1,0:T(8,128)S(1)} %multiply_reduce_fusion.25, f32[32,256]{1,0:T(8,128)S(1)} %multiply_reduce_fusion.26, ...), kind=kOutput, calls=%fused_computation.29.clone.1 | convolution fusion | flops 1630535680 | bytes 12649120 | tf_op jit(solution)/shard_map/while/body/eval_jaxpr/nbq,bqp->bnp/dot_general | solution.py:32
  312.0 13.6 %bitcast_dynamic-update-slice_fusion.4 = f32[8,32,64,256]{3,2,1,0:T(8,128)} fusion(f32[8,32,64,256]{3,2,1,0:T(8,128)} %get-tuple-element.347, s32[]{:T(128)} %get-tuple-element.346, f32[32,256,256]{2,1,0:T(8,128)} %fusion.413, f32[32,256]{1,0:T(8,128)S(1)} %multiply_reduce_fusion.25, f32[32,256]{1,0:T(8,128)S(1)} %multiply_reduce_fusion.26, ...), kind=kOutput, calls=%fused_computation.29.clone.1 | convolution fusion | flops 1630535680 | bytes 12649120 | tf_op jit(solution)/shard_map/while/body/eval_jaxpr/nbq,bqp->bnp/dot_general | solution.py:32
  340.0 13.6 %bitcast_dynamic-update-slice_fusion.4 = f32[8,32,64,256]{3,2,1,0:T(8,128)} fusion(f32[8,32,64,256]{3,2,1,0:T(8,128)} %get-tuple-element.347, s32[]{:T(128)} %get-tuple-element.346, f32[32,256,256]{2,1,0:T(8,128)} %fusion.413, f32[32,256]{1,0:T(8,128)S(1)} %multiply_reduce_fusion.25, f32[32,256]{1,0:T(8,128)S(1)} %multiply_reduce_fusion.26, ...), kind=kOutput, calls=%fused_computation.29.clone.1 | convolution fusion | flops 1630535680 | bytes 12649120 | tf_op jit(solution)/shard_map/while/body/eval_jaxpr/nbq,bqp->bnp/dot_general | solution.py:32
  354.0 9.4 %reduce_sum.221 = f32[32,64,256]{2,1,0:T(8,128)} reduce(f32[32,8,64,256]{3,2,1,0:T(8,128)} %bitcast.261, f32[]{:T(128)} %constant.298.clone.1), dimensions={1}, to_apply=%region_6.9 | reduce | flops 3670016 | bytes 18874372 | tf_op jit(solution)/shard_map/reduce_sum | solution.py:163
  370.4 63.4 %all-reduce = (f32[64]{0:T(128)S(1)}, f32[64]{0:T(128)S(1)}) all-reduce(f32[64]{0:T(128)S(1)} %copy-done.29, f32[64]{0:T(128)S(1)} %multiply_reduce_fusion.5), channel_id=1, replica_groups=mesh['leaf'=32,'sub'=4] {'leaf','sub'}, use_global_device_ids=true, to_apply=%region_1.0 | all-reduce | flops 128 | bytes 1024 | tf_op jit(solution)/shard_map/psum | solution.py:172
  437.8 64.5 %psum.23 = f32[64]{0:T(128)S(1)} all-reduce(f32[64]{0:T(128)S(1)} %get-tuple-element.178), channel_id=1, replica_groups=mesh['leaf'=32,'sub'=4] {'leaf','sub'}, use_global_device_ids=true, to_apply=%region_25.30 | all-reduce | flops 64 | bytes 512 | tf_op jit(solution)/shard_map/psum | solution.py:178
  567.2 18.7 %bitcast_reduce_fusion = f32[32,64,64]{2,1,0:T(8,128)} fusion(f32[256]{0:T(256)S(1)} %reshape.510, f32[256,64,64]{2,1,0:T(8,128)} %exponential_multiply_fusion, f32[256,64,64]{1,2,0:T(8,128)} %gather_fusion.9, pred[256]{0:T(512)(128)(4,1)S(1)} %copy-done.28), kind=kOutput, calls=%fused_computation.112 | convolution fusion | flops 808321024 | bytes 8914176 | tf_op jit(solution)/shard_map/bij,bjn->bin/dot_general | solution.py:59
  600.7 224.9 %while.21 = (s32[]{:T(128)}, f32[8,32,64,256]{3,2,1,0:T(8,128)}, s32[8,32]{1,0:T(8,128)S(1)}, f32[64,64,256]{2,0,1:T(8,128)}, f32[64,8,256]{2,1,0:T(8,128)S(1)},...) while((s32[]{:T(128)}, f32[8,32,64,256]{3,2,1,0:T(8,128)}, s32[8,32]{1,0:T(8,128)S(1)}, ...), condition=%wide.region_29.34_spmd, body=%wide.region_26.33_spmd.sunk | while | flops 1832372608 | bytes 27404604 | solution.py:48
  602.2 9.3 %fusion.419 = f32[32,256,256]{2,1,0:T(8,128)} fusion(f32[32,8,256]{2,1,0:T(8,128)S(1)} %gather_fusion.3, f32[32,8,256]{2,1,0:T(8,128)S(1)} %gather_fusion.4, pred[32]{0:T(512)(128)(4,1)S(1)} %get-tuple-element.336, pred[32]{0:T(512)(128)(4,1)S(1)} %get-tuple-element.337), kind=kOutput, calls=%fused_computation.87.clone.1 | convolution fusion | flops 201457664 | bytes 8912960 | tf_op jit(solution)/shard_map/while/body/eval_jaxpr/bdm,bdn->bmn/dot_general | solution.py:19
  615.4 13.6 %bitcast_dynamic-update-slice_fusion.5 = f32[8,32,64,256]{3,2,1,0:T(8,128)} fusion(f32[8,32,64,256]{3,2,1,0:T(8,128)} %get-tuple-element.371, s32[]{:T(128)} %get-tuple-element.370, f32[32,256,256]{2,1,0:T(8,128)} %fusion.419, f32[32,256]{1,0:T(8,128)S(1)} %multiply_reduce_fusion.27, f32[32,256]{1,0:T(8,128)S(1)} %multiply_reduce_fusion.28, ...), kind=kOutput, calls=%fused_computation.80.clone.1 | convolution fusion | flops 1630535680 | bytes 12649120 | tf_op jit(solution)/shard_map/while/body/eval_jaxpr/nbq,bqp->bnp/dot_general | solution.py:32
  643.5 13.6 %bitcast_dynamic-update-slice_fusion.5 = f32[8,32,64,256]{3,2,1,0:T(8,128)} fusion(f32[8,32,64,256]{3,2,1,0:T(8,128)} %get-tuple-element.371, s32[]{:T(128)} %get-tuple-element.370, f32[32,256,256]{2,1,0:T(8,128)} %fusion.419, f32[32,256]{1,0:T(8,128)S(1)} %multiply_reduce_fusion.27, f32[32,256]{1,0:T(8,128)S(1)} %multiply_reduce_fusion.28, ...), kind=kOutput, calls=%fused_computation.80.clone.1 | convolution fusion | flops 1630535680 | bytes 12649120 | tf_op jit(solution)/shard_map/while/body/eval_jaxpr/nbq,bqp->bnp/dot_general | solution.py:32
  658.3 9.3 %fusion.419 = f32[32,256,256]{2,1,0:T(8,128)} fusion(f32[32,8,256]{2,1,0:T(8,128)S(1)} %gather_fusion.3, f32[32,8,256]{2,1,0:T(8,128)S(1)} %gather_fusion.4, pred[32]{0:T(512)(128)(4,1)S(1)} %get-tuple-element.336, pred[32]{0:T(512)(128)(4,1)S(1)} %get-tuple-element.337), kind=kOutput, calls=%fused_computation.87.clone.1 | convolution fusion | flops 201457664 | bytes 8912960 | tf_op jit(solution)/shard_map/while/body/eval_jaxpr/bdm,bdn->bmn/dot_general | solution.py:19
  671.5 13.6 %bitcast_dynamic-update-slice_fusion.5 = f32[8,32,64,256]{3,2,1,0:T(8,128)} fusion(f32[8,32,64,256]{3,2,1,0:T(8,128)} %get-tuple-element.371, s32[]{:T(128)} %get-tuple-element.370, f32[32,256,256]{2,1,0:T(8,128)} %fusion.419, f32[32,256]{1,0:T(8,128)S(1)} %multiply_reduce_fusion.27, f32[32,256]{1,0:T(8,128)S(1)} %multiply_reduce_fusion.28, ...), kind=kOutput, calls=%fused_computation.80.clone.1 | convolution fusion | flops 1630535680 | bytes 12649120 | tf_op jit(solution)/shard_map/while/body/eval_jaxpr/nbq,bqp->bnp/dot_general | solution.py:32
  686.4 9.3 %fusion.419 = f32[32,256,256]{2,1,0:T(8,128)} fusion(f32[32,8,256]{2,1,0:T(8,128)S(1)} %gather_fusion.3, f32[32,8,256]{2,1,0:T(8,128)S(1)} %gather_fusion.4, pred[32]{0:T(512)(128)(4,1)S(1)} %get-tuple-element.336, pred[32]{0:T(512)(128)(4,1)S(1)} %get-tuple-element.337), kind=kOutput, calls=%fused_computation.87.clone.1 | convolution fusion | flops 201457664 | bytes 8912960 | tf_op jit(solution)/shard_map/while/body/eval_jaxpr/bdm,bdn->bmn/dot_general | solution.py:19
  699.6 13.6 %bitcast_dynamic-update-slice_fusion.5 = f32[8,32,64,256]{3,2,1,0:T(8,128)} fusion(f32[8,32,64,256]{3,2,1,0:T(8,128)} %get-tuple-element.371, s32[]{:T(128)} %get-tuple-element.370, f32[32,256,256]{2,1,0:T(8,128)} %fusion.419, f32[32,256]{1,0:T(8,128)S(1)} %multiply_reduce_fusion.27, f32[32,256]{1,0:T(8,128)S(1)} %multiply_reduce_fusion.28, ...), kind=kOutput, calls=%fused_computation.80.clone.1 | convolution fusion | flops 1630535680 | bytes 12649120 | tf_op jit(solution)/shard_map/while/body/eval_jaxpr/nbq,bqp->bnp/dot_general | solution.py:32
  714.4 9.3 %fusion.419 = f32[32,256,256]{2,1,0:T(8,128)} fusion(f32[32,8,256]{2,1,0:T(8,128)S(1)} %gather_fusion.3, f32[32,8,256]{2,1,0:T(8,128)S(1)} %gather_fusion.4, pred[32]{0:T(512)(128)(4,1)S(1)} %get-tuple-element.336, pred[32]{0:T(512)(128)(4,1)S(1)} %get-tuple-element.337), kind=kOutput, calls=%fused_computation.87.clone.1 | convolution fusion | flops 201457664 | bytes 8912960 | tf_op jit(solution)/shard_map/while/body/eval_jaxpr/bdm,bdn->bmn/dot_general | solution.py:19
  727.7 13.6 %bitcast_dynamic-update-slice_fusion.5 = f32[8,32,64,256]{3,2,1,0:T(8,128)} fusion(f32[8,32,64,256]{3,2,1,0:T(8,128)} %get-tuple-element.371, s32[]{:T(128)} %get-tuple-element.370, f32[32,256,256]{2,1,0:T(8,128)} %fusion.419, f32[32,256]{1,0:T(8,128)S(1)} %multiply_reduce_fusion.27, f32[32,256]{1,0:T(8,128)S(1)} %multiply_reduce_fusion.28, ...), kind=kOutput, calls=%fused_computation.80.clone.1 | convolution fusion | flops 1630535680 | bytes 12649120 | tf_op jit(solution)/shard_map/while/body/eval_jaxpr/nbq,bqp->bnp/dot_general | solution.py:32
  742.5 9.3 %fusion.419 = f32[32,256,256]{2,1,0:T(8,128)} fusion(f32[32,8,256]{2,1,0:T(8,128)S(1)} %gather_fusion.3, f32[32,8,256]{2,1,0:T(8,128)S(1)} %gather_fusion.4, pred[32]{0:T(512)(128)(4,1)S(1)} %get-tuple-element.336, pred[32]{0:T(512)(128)(4,1)S(1)} %get-tuple-element.337), kind=kOutput, calls=%fused_computation.87.clone.1 | convolution fusion | flops 201457664 | bytes 8912960 | tf_op jit(solution)/shard_map/while/body/eval_jaxpr/bdm,bdn->bmn/dot_general | solution.py:19
  755.7 13.6 %bitcast_dynamic-update-slice_fusion.5 = f32[8,32,64,256]{3,2,1,0:T(8,128)} fusion(f32[8,32,64,256]{3,2,1,0:T(8,128)} %get-tuple-element.371, s32[]{:T(128)} %get-tuple-element.370, f32[32,256,256]{2,1,0:T(8,128)} %fusion.419, f32[32,256]{1,0:T(8,128)S(1)} %multiply_reduce_fusion.27, f32[32,256]{1,0:T(8,128)S(1)} %multiply_reduce_fusion.28, ...), kind=kOutput, calls=%fused_computation.80.clone.1 | convolution fusion | flops 1630535680 | bytes 12649120 | tf_op jit(solution)/shard_map/while/body/eval_jaxpr/nbq,bqp->bnp/dot_general | solution.py:32
  770.5 9.3 %fusion.419 = f32[32,256,256]{2,1,0:T(8,128)} fusion(f32[32,8,256]{2,1,0:T(8,128)S(1)} %gather_fusion.3, f32[32,8,256]{2,1,0:T(8,128)S(1)} %gather_fusion.4, pred[32]{0:T(512)(128)(4,1)S(1)} %get-tuple-element.336, pred[32]{0:T(512)(128)(4,1)S(1)} %get-tuple-element.337), kind=kOutput, calls=%fused_computation.87.clone.1 | convolution fusion | flops 201457664 | bytes 8912960 | tf_op jit(solution)/shard_map/while/body/eval_jaxpr/bdm,bdn->bmn/dot_general | solution.py:19
  783.8 13.6 %bitcast_dynamic-update-slice_fusion.5 = f32[8,32,64,256]{3,2,1,0:T(8,128)} fusion(f32[8,32,64,256]{3,2,1,0:T(8,128)} %get-tuple-element.371, s32[]{:T(128)} %get-tuple-element.370, f32[32,256,256]{2,1,0:T(8,128)} %fusion.419, f32[32,256]{1,0:T(8,128)S(1)} %multiply_reduce_fusion.27, f32[32,256]{1,0:T(8,128)S(1)} %multiply_reduce_fusion.28, ...), kind=kOutput, calls=%fused_computation.80.clone.1 | convolution fusion | flops 1630535680 | bytes 12649120 | tf_op jit(solution)/shard_map/while/body/eval_jaxpr/nbq,bqp->bnp/dot_general | solution.py:32
  798.6 9.3 %fusion.419 = f32[32,256,256]{2,1,0:T(8,128)} fusion(f32[32,8,256]{2,1,0:T(8,128)S(1)} %gather_fusion.3, f32[32,8,256]{2,1,0:T(8,128)S(1)} %gather_fusion.4, pred[32]{0:T(512)(128)(4,1)S(1)} %get-tuple-element.336, pred[32]{0:T(512)(128)(4,1)S(1)} %get-tuple-element.337), kind=kOutput, calls=%fused_computation.87.clone.1 | convolution fusion | flops 201457664 | bytes 8912960 | tf_op jit(solution)/shard_map/while/body/eval_jaxpr/bdm,bdn->bmn/dot_general | solution.py:19
  811.8 13.6 %bitcast_dynamic-update-slice_fusion.5 = f32[8,32,64,256]{3,2,1,0:T(8,128)} fusion(f32[8,32,64,256]{3,2,1,0:T(8,128)} %get-tuple-element.371, s32[]{:T(128)} %get-tuple-element.370, f32[32,256,256]{2,1,0:T(8,128)} %fusion.419, f32[32,256]{1,0:T(8,128)S(1)} %multiply_reduce_fusion.27, f32[32,256]{1,0:T(8,128)S(1)} %multiply_reduce_fusion.28, ...), kind=kOutput, calls=%fused_computation.80.clone.1 | convolution fusion | flops 1630535680 | bytes 12649120 | tf_op jit(solution)/shard_map/while/body/eval_jaxpr/nbq,bqp->bnp/dot_general | solution.py:32
  825.6 9.4 %reduce_sum.256 = f32[32,64,256]{2,1,0:T(8,128)} reduce(f32[32,8,64,256]{3,2,1,0:T(8,128)} %bitcast.262, f32[]{:T(128)} %constant.298.clone.1), dimensions={1}, to_apply=%region_30.35 | reduce | flops 3670016 | bytes 18874372 | tf_op jit(solution)/shard_map/reduce_sum | solution.py:163
  (360 shorter events, 345.2 us)
Async XLA Ops:
  5.1 15.3 %copy-start.9 = (f32[32,64,64]{2,1,0:T(8,128)}, f32[32,64,64]{2,1,0:T(8,128)S(1)}, u32[]{:S(2)}) copy-start(f32[32,64,64]{2,1,0:T(8,128)S(1)} %fusion.103) | copy-start | bytes 1572868
  5.2 79.0 %collective-permute-start.10 = (f32[32,64,64]{2,1,0:T(8,128)S(1)}, f32[32,64,64]{2,1,0:T(8,128)}, u32[]{:S(2)}, u32[]{:S(2)}) collective-permute-start(f32[32,64,64]{2,1,0:T(8,128)S(1)} %fusion.103), channel_id=1, source_target_pairs={{0,4},{4,0},{8,12},{12,8},{16,20},{20,16},{24,28},{28,24},{32,36},... | collective-permute-start | bytes 1572872 | tf_op jit(solution)/shard_map/ppermute | solution.py:15
  7.1 7.8 collective-permute-start.2
  7.6 29.0 %collective-permute-start.9 = (f32[8,2048]{1,0:T(8,128)S(1)}, f32[8,2048]{1,0:T(8,128)S(1)}, u32[]{:S(2)}, u32[]{:S(2)}) collective-permute-start(f32[8,2048]{1,0:T(8,128)S(1)} %copy-done.24), channel_id=1, source_target_pairs={{0,4},{4,0},{8,12},{12,8},{16,20},{20,16},{24,28},{28,24},{32,36},... | collective-permute-start | bytes 196616 | tf_op jit(solution)/shard_map/ppermute | solution.py:15
  9.7 104.8 %collective-permute-start = (f32[64,32,256]{2,1,0:T(8,128)}, f32[64,32,256]{2,1,0:T(8,128)}, u32[]{:S(2)}, u32[]{:S(2)}) collective-permute-start(f32[64,32,256]{2,1,0:T(8,128)} %bitcast.65), channel_id=1, source_target_pairs={{0,4},{4,0},{8,12},{12,8},{16,20},{20,16},{24,28},{28,24},{32,36},... | collective-permute-start | bytes 6291464 | tf_op jit(solution)/shard_map/ppermute | solution.py:15
  10.1 73.0 %collective-permute-start.1 = (f32[8,8192]{1,0:T(8,128)S(1)}, f32[8,8192]{1,0:T(8,128)}, u32[]{:S(2)}, u32[]{:S(2)}) collective-permute-start(f32[8,8192]{1,0:T(8,128)S(1)} %copy-done.12), channel_id=1, source_target_pairs={{0,4},{4,0},{8,12},{12,8},{16,20},{20,16},{24,28},{28,24},{32,36},... | collective-permute-start | bytes 786440 | tf_op jit(solution)/shard_map/ppermute | solution.py:15
  15.9 4.5 collective-permute-start.3
  20.4 9.8 %copy-start.18 = (f32[64,64]{0,1:T(8,128)}, f32[64,64]{0,1:T(8,128)S(1)}, u32[]{:S(2)}) copy-start(f32[64,64]{0,1:T(8,128)S(1)} %collective-permute-done.3) | copy-start | bytes 49156
  21.4 5.6 collective-permute-start.4
  28.0 4.0 collective-permute-start.5
  33.6 7.5 collective-permute-start.6
  42.2 4.0 collective-permute-start.7
  47.2 26.8 %copy-start.16 = (f32[64,64]{1,0:T(8,128)S(1)}, f32[64,64]{1,0:T(8,128)}, u32[]{:S(2)}) copy-start(f32[64,64]{1,0:T(8,128)} %exponential_multiply_fusion.5) | copy-start | bytes 49156
  47.2 28.1 %copy-start.14 = (f32[64,64]{1,0:T(8,128)S(1)}, f32[64,64]{1,0:T(8,128)}, u32[]{:S(2)}) copy-start(f32[64,64]{1,0:T(8,128)} %exponential_multiply_fusion.4) | copy-start | bytes 49156
  47.2 30.1 %copy-start.23 = (f32[64,64]{0,1:T(8,128)S(1)}, f32[64,64]{0,1:T(8,128)}, u32[]{:S(2)}) copy-start(f32[64,64]{0,1:T(8,128)} %copy-done.22) | copy-start | bytes 49156
  47.2 31.4 %copy-start.21 = (f32[64,64]{0,1:T(8,128)S(1)}, f32[64,64]{0,1:T(8,128)}, u32[]{:S(2)}) copy-start(f32[64,64]{0,1:T(8,128)} %copy-done.20) | copy-start | bytes 49156
  47.3 32.7 %copy-start.19 = (f32[64,64]{0,1:T(8,128)S(1)}, f32[64,64]{0,1:T(8,128)}, u32[]{:S(2)}) copy-start(f32[64,64]{0,1:T(8,128)} %copy-done.18) | copy-start | bytes 49156
  47.3 25.5 %collective-permute-start.8 = (f32[64,64]{1,0:T(8,128)S(1)}, f32[64,64]{1,0:T(8,128)S(1)}, u32[]{:S(2)}, u32[]{:S(2)}) collective-permute-start(f32[64,64]{1,0:T(8,128)S(1)} %fusion.184), channel_id=1, source_target_pairs={{0,2},{1,3},{2,0},{3,1},{4,6},{5,7},{6,4},{7,5},{8,10},{9,11},{10,... | collective-permute-start | bytes 49160 | tf_op jit(solution)/shard_map/ppermute | solution.py:15
  354.0 9.4 %copy-start.3 = (f32[64,8192]{1,0:T(8,128)S(1)}, f32[64,8192]{1,0:T(8,128)}, u32[]{:S(2)}) copy-start(f32[64,8192]{1,0:T(8,128)} %param.27) | copy-start | bytes 6291460
  511.2 36.6 %copy-start.7 = (f32[64,8192]{1,0:T(8,128)S(1)}, f32[64,8192]{1,0:T(8,128)}, u32[]{:S(2)}) copy-start(f32[64,8192]{1,0:T(8,128)} %copy-done.6) | copy-start | bytes 6291460
  511.2 41.6 %copy-start.17 = (f32[64,64]{1,0:T(8,128)S(1)}, f32[64,64]{1,0:T(8,128)}, u32[]{:S(2)}) copy-start(f32[64,64]{1,0:T(8,128)} %exponential_multiply_fusion.5) | copy-start | bytes 49156
  511.2 42.8 %copy-start.15 = (f32[64,64]{1,0:T(8,128)S(1)}, f32[64,64]{1,0:T(8,128)}, u32[]{:S(2)}) copy-start(f32[64,64]{1,0:T(8,128)} %exponential_multiply_fusion.4) | copy-start | bytes 49156
  515.4 1.5 collective-permute-start.12
  517.8 4.0 collective-permute-start.13
  522.8 5.5 collective-permute-start.14
  529.3 4.2 collective-permute-start.15
  534.5 5.5 collective-permute-start.16
  541.0 4.0 collective-permute-start.17
  546.0 5.5 collective-permute-start.18
  547.8 13.4 %collective-permute-start.19 = (f32[32,64,64]{1,2,0:T(8,128)}, f32[32,64,64]{1,2,0:T(8,128)}, u32[]{:S(2)}, u32[]{:S(2)}) collective-permute-start(f32[32,64,64]{1,2,0:T(8,128)} %copy-done.10), channel_id=1, source_target_pairs={{0,4},{4,0},{8,12},{12,8},{16,20},{20,16},{24,28},{28,24},{32,36},... | collective-permute-start | bytes 1572872 | tf_op jit(solution)/shard_map/ppermute | solution.py:15
  549.8 36.2 %collective-permute-start.11 = (f32[64,32,256]{2,1,0:T(8,128)}, f32[64,32,256]{2,1,0:T(8,128)}, u32[]{:S(2)}, u32[]{:S(2)}) collective-permute-start(f32[64,32,256]{2,1,0:T(8,128)} %bitcast.67), channel_id=1, source_target_pairs={{0,4},{4,0},{8,12},{12,8},{16,20},{20,16},{24,28},{28,24},{32,36},... | collective-permute-start | bytes 6291464 | tf_op jit(solution)/shard_map/ppermute | solution.py:15
  825.6 9.4 %copy-start.5 = (f32[64,8192]{1,0:T(8,128)S(1)}, f32[64,8192]{1,0:T(8,128)}, u32[]{:S(2)}) copy-start(f32[64,8192]{1,0:T(8,128)} %param.30) | copy-start | bytes 6291460
  (18 other events, 71.8 us)
where the time goes:
time: 855 us; the launch traced here: 844 us
  matrix products  484 us (57%)
  local copies, waits for them, and re-layouts  129 us (15%)
  blocking collectives  128 us (15%)
  other arithmetic  50.7 us (6%)
  waiting for transfers between devices  25.1 us (3%)
  starting transfers between devices  22.9 us (3%)
    dot_general x16, matrix products, near_block(): terms = jnp.einsum('nbq,bqp->bnp', source_vec, kernel, precision=highest)  218 us
    dot_general x23, matrix products, matern(): cross = jnp.einsum('bdm,bdn->bmn', first_pts, second_pts, precision=highest)  174 us
    psum x1, blocking collectives, shards(): lax.psum(jnp.sum(new_residual * new_residual, axis=1), ('leaf', 'sub'))  64.5 us
    psum x1, blocking collectives, shards(): norm_old = lax.psum(jnp.sum(residual * residual, axis=1), ('leaf', 'sub'))  63.4 us
    gather x16, local copies, waits for them, and re-layouts, near_block(): source_vec = jnp.take(vector_tab, sources, axis=1)  45.9 us
    dot_general x2, matrix products, far_terms(): jnp.einsum('bij,bjn->bin', kernel, jnp.take(weight_tab, sources, axis=0),...  43 us
    ppermute x20, waiting for transfers between devices, from_partner(): lax.ppermute(value, axis, [(i, i ^ 1 << apart) for i in range(lax.axis_si...  25.1 us
    ppermute x20, starting transfers between devices, from_partner(): lax.ppermute(value, axis, [(i, i ^ 1 << apart) for i in range(lax.axis_si...  22.9 us
  transfers between devices with their start and end apart: 20, of which 10 were waited for; matrix products, arithmetic and copies ran while one was open for 15% of the time, Pallas kernels for 0%

commit v1 on v0

v1 whole, which is shorter than its diff:
```python
import functools
import math

import jax
import jax.numpy as jnp
from jax import lax
from jax.experimental import pallas as pl
from jax.experimental.pallas import tpu as pltpu
from jax.sharding import PartitionSpec as P

MESH = pl.DeviceIdType.MESH
f32, bf16 = jnp.float32, jnp.bfloat16
noise_level = 1.0
amplitude = 0.1
length_scale = 1.0
LN2 = math.log(2.0)
COORD = math.sqrt(3.0) / length_scale / LN2
LEAVES, LEAF, RANK, COLS = 32, 256, 64, 64
SLOTS, BUFS, AHEAD = 200, 8, 4
CORE = (1,)
RINGS = ((2, 4, 6), (8, 16, 24), (32, 64, 96))


def dot(a, b):
    return lax.dot_general(a, b, (((1,), (0,)), ((), ())), preferred_element_type=f32)


def dot_nt(a, b):
    return lax.dot_general(a, b, (((1,), (1,)), ((), ())), preferred_element_type=f32)


def split(a):
    hi = a.astype(bf16)
    return hi, (a - hi.astype(f32)).astype(bf16)


def dot3(a, b):
    ah, al = split(a)
    bh, bl = split(b)
    return dot(ah, bh) + (dot(ah, bl) + dot(al, bh))


def kern(u):
    t = jnp.maximum(u, 1e-12)
    s = t * lax.rsqrt(t)
    return (amplitude + (amplitude * LN2) * s) * jnp.exp2(-s)


def pieces(a):
    one = a.astype(bf16).astype(f32)
    rest = a - one
    two = rest.astype(bf16).astype(f32)
    three = (rest - two).astype(bf16).astype(f32)
    return one, two, three


def features(coords):
    a = coords * COORD
    a1, a2, a3 = pieces(a)
    n1, n2, n3 = pieces(jnp.sum(a * a, axis=0, keepdims=True))
    row = lax.broadcasted_iota(jnp.int32, a.shape, 0)
    norm = jnp.where((row == 0) | (row == 3), n1, jnp.where((row == 1) | (row == 4), n2, n3))
    zero = jnp.zeros_like(a)
    src_norm = jnp.where(row < 3, norm, jnp.where(row < 6, 1.0, 0.0))
    tgt_norm = jnp.where(row < 3, 1.0, jnp.where(row < 6, norm, 0.0))
    s1, s2, s3 = -2.0 * a1, -2.0 * a2, -2.0 * a3
    source = jnp.concatenate([s1, s1, s2, s2, s1, s3, src_norm, zero], axis=0)
    target = jnp.concatenate([a1, a2, a1, a2, a3, a1, tgt_norm, zero], axis=0)
    return source, target


def tree_position():
    return lax.axis_index("sub") * 32 + lax.axis_index("leaf")


def device_at(q):
    return (lax.rem(q, 32), lax.div(q, 32))


def greet(masks):
    q = tree_position()
    barrier = pltpu.get_barrier_semaphore()
    for mask in masks:
        pl.semaphore_signal(barrier, inc=1, device_id=device_at(q ^ mask), device_id_type=MESH)


def await_greetings(masks):
    pl.semaphore_wait(pltpu.get_barrier_semaphore(), len(masks))


def exchange(buf, number, masks, send, recv):
    q = tree_position()
    return [
        pltpu.make_async_remote_copy(
            buf.at[number, 0],
            buf.at[number, i + 1],
            send.at[number, i],
            recv.at[number, i],
            device_id=device_at(q ^ mask),
            device_id_type=MESH,
        )
        for i, mask in enumerate(masks)
    ]


def climb_kernel(
    d, x, lb, db, transfer, nc, pts, sk,
    z0, w_own, dp, xp, wp, ptp, skp,
    mats, kmask, buf, mat_sem, far_send, far_recv, send, recv,
):
    q = tree_position()
    every = CORE + sum(RINGS, ())
    greet(every)
    spots = []
    for c in range(1, 7):
        base = 128 - 2 * (128 >> c)
        node = lax.shift_right_logical(q, c)
        if c % 2:
            spots.append((base + node, 1, (c - 1) // 2 * 3))
        else:
            spots.append((base + (node & -2), 2, (c - 2) // 2 * 3 + 1))
    loads = [
        pltpu.make_async_copy(transfer.at[pl.ds(at, n)], mats.at[pl.ds(slot, n)], mat_sem.at[i])
        for i, (at, n, slot) in enumerate(spots)
    ]
    for load in loads:
        load.start()
    await_greetings(every)
    partner = device_at(q ^ 1)
    bulk = [
        pltpu.make_async_remote_copy(
            a, b, far_send.at[i], far_recv.at[i], device_id=partner, device_id_type=MESH
        )
        for i, (a, b) in enumerate(((d, dp), (x, xp), (pts, ptp), (sk, skp), (w_own, wp)))
    ]
    for copy in bulk[:4]:
        copy.start()

    def leaf(l, carry):
        at = pl.ds(pl.multiple_of(l * LEAF, LEAF), LEAF)
        vh, vl = split(jnp.concatenate([d[:, at], x[:, at]], axis=0))
        bh, bl = split(lb[:, at])
        both = dot_nt(jnp.concatenate([bh, bl], axis=0), vh)
        w_own[pl.ds(pl.multiple_of(l * RANK, RANK), RANK), :] = (
            both[:RANK] + both[RANK:] + dot_nt(bh, vl)
        )
        return carry

    lax.fori_loop(0, LEAVES, leaf, 0, unroll=4)
    bulk[4].start()
    buf[0, 0] = dot3(db[...], w_own[...])
    core = exchange(buf, 0, CORE, send, recv)
    for copy in core:
        copy.start()
    row = lax.broadcasted_iota(jnp.int32, (128, 128), 0)
    col = lax.broadcasted_iota(jnp.int32, (128, 128), 1)
    for c in range(1, 7):
        start = 64 * (128 - 2 * (128 >> c)) + 128 * lax.shift_right_logical(q, c + 1)
        source, target = features(nc[:, pl.ds(pl.multiple_of(start, 128), 128)])
        full = kern(dot(source.T.astype(bf16), target.astype(bf16)))
        kmask[c - 1] = jnp.where((row < 64) == (col < 64), 0.0, full)
    for load in loads:
        load.wait()

    def own_pair(number, a):
        e = a & 2
        return jnp.concatenate([buf[number, a ^ e], buf[number, a ^ (e + 1)]], axis=0)

    def pair(number, a, b):
        return jnp.concatenate([buf[number, a ^ (2 * b)], buf[number, a ^ (2 * b + 1)]], axis=0)

    stacks = [None] * 7
    for copy in core:
        copy.wait()
    h = q & 1
    bottom = jnp.concatenate([buf[0, h], buf[0, h ^ 1]], axis=0)
    current = dot3(mats[0], bottom)
    for r in range(3):
        buf[r + 1, 0] = current
        copies = exchange(buf, r + 1, RINGS[r], send, recv)
        for copy in copies:
            copy.start()
        for copy in copies:
            copy.wait()
        a = lax.shift_right_logical(q, 2 * r + 1) & 3
        stacks[2 * r + 1] = own_pair(r + 1, a)
        stacks[2 * r + 2] = jnp.concatenate(
            [dot3(mats[3 * r + 1 + b], pair(r + 1, a, b)) for b in range(2)], axis=0
        )
        if r < 2:
            current = dot3(mats[3 * r + 3], stacks[2 * r + 2])

    def half(value, c):
        return jnp.where((lax.shift_right_logical(q, c) & 1) == 0, value[:64], value[64:])

    down = half(dot3(kmask[5], stacks[6]), 6)
    for c in range(6, 0, -1):
        if c % 2:
            matrix = mats[(c - 1) // 2 * 3]
        else:
            matrix = mats[(c - 2) // 2 * 3 + 1 + (lax.shift_right_logical(q, c) & 1)]
        children = dot3(matrix.T, down)
        if c > 1:
            children = children + dot3(kmask[c - 2], stacks[c - 1])
        down = half(children, c - 1)
    z0[...] = down
    for copy in bulk:
        copy.wait()


def apply_kernel(
    count, tg, sr, far, d, x, dp, xp, pts, ptp, sk, skp, w_own, wp, lb, db, z0, res,
    hd, hx, sums,
    vt, fs, ft, wt, fte, fto, fsk, zl, acc, kh, kl,
):
    def leaf_tables(l, carry):
        at = pl.ds(pl.multiple_of(l * LEAF, LEAF), LEAF)
        for side, (dd, xx, pp) in enumerate(((d, x, pts), (dp, xp, ptp))):
            hi, lo = split(jnp.concatenate([dd[:, at], xx[:, at]], axis=0))
            vt[side * LEAVES + l] = jnp.concatenate([hi, lo], axis=0)
            source, target = features(pp[:, at])
            fs[side * LEAVES + l] = source.T.astype(bf16)
            if side == 0:
                ft[l] = target.astype(bf16)
        acc[l] = jnp.zeros((2 * COLS, LEAF), f32)
        return carry

    lax.fori_loop(0, LEAVES, leaf_tables, 0, unroll=2)
    vt[2 * LEAVES] = jnp.zeros((4 * COLS, LEAF), bf16)
    fs[2 * LEAVES] = jnp.zeros((LEAF, 64), bf16)
    wt[2 * LEAVES] = jnp.zeros((RANK, 4 * COLS), bf16)
    fte[2 * LEAVES] = jnp.zeros((64, 128), bf16)
    fto[2 * LEAVES] = jnp.zeros((64, 128), bf16)

    def skel_tables(m, carry):
        at = pl.ds(pl.multiple_of(m * 128, 128), 128)
        low = lax.broadcasted_iota(jnp.int32, (64, 128), 1) < 64
        for side, (ss, ww) in enumerate(((sk, w_own), (skp, wp))):
            source, target = features(ss[:, at])
            turned = pltpu.roll(target, 64, 1)
            one = side * LEAVES + 2 * m
            fte[one] = jnp.where(low, target, 0.0).astype(bf16)
            fto[one] = jnp.where(low, 0.0, turned).astype(bf16)
            fte[one + 1] = jnp.where(low, turned, 0.0).astype(bf16)
            fto[one + 1] = jnp.where(low, 0.0, target).astype(bf16)
            for i in range(2):
                hi, lo = split(ww[pl.ds(pl.multiple_of(m * 128 + i * 64, 64), 64), :])
                wt[one + i] = jnp.concatenate([hi, lo], axis=1)
            if side == 0:
                flipped = source.T.astype(bf16)
                fsk[2 * m] = flipped[:64]
                fsk[2 * m + 1] = flipped[64:]
        dh, dl = split(db[:, at].T)
        zh, zlo = split(z0[...])
        part = dot(dh, zh) + (dot(dh, zlo) + dot(dl, zh))
        zl[2 * m] = part[:64]
        zl[2 * m + 1] = part[64:]
        return carry

    lax.fori_loop(0, LEAVES // 2, skel_tables, 0, unroll=2)

    def tile(k, b):
        hi, lo = split(kern(dot(fs[sr[k]], ft[tg[k]])))
        kh[b] = hi
        kl[b] = lo

    def multiply(k, b):
        v = vt[sr[k]]
        both = dot(v, kh[b])
        acc[tg[k]] += both[: 2 * COLS] + both[2 * COLS :] + dot(v[: 2 * COLS], kl[b])

    for j in range(AHEAD):
        tile(j, j)

    def near(i, carry):
        for j in range(BUFS):
            k = i * BUFS + j
            multiply(k, j)
            tile(jnp.minimum(k + AHEAD, SLOTS - 1), (j + AHEAD) % BUFS)
        return carry

    lax.fori_loop(0, lax.div(count[0] + (BUFS - 1), BUFS), near, 0)

    def finish(l, carry):
        lanes = []
        rows = []
        for j in range(4):
            one, two = far[l * 8 + 2 * j], far[l * 8 + 2 * j + 1]
            lanes.append(fte[one] + fto[two])
            rows += [wt[one], wt[two]]
        kk = kern(dot(fsk[l], jnp.concatenate(lanes, axis=1)))
        hi, lo = split(kk)
        got = dot(jnp.concatenate([hi, lo], axis=0), jnp.concatenate(rows, axis=0))
        z = zl[l] + got[:64, :128] + got[:64, 128:] + got[64:, :128]
        zh = z.astype(bf16).astype(f32)
        zcat = jnp.concatenate([zh, z - zh, zh], axis=0).T.astype(bf16)
        at = pl.ds(pl.multiple_of(l * LEAF, LEAF), LEAF)
        bh, bl = split(lb[:, at])
        out = acc[l] + dot(zcat, jnp.concatenate([bh, bh, bl], axis=0))
        dl = d[:, at]
        image = noise_level * dl + out[:COLS]
        hd[:, at] = image
        hx[:, at] = noise_level * x[:, at] + out[COLS:]
        r = res[:, at]

        def fold(value):
            return value[:, :128] + value[:, 128:]

        curv, cross, square, old = carry
        return (
            curv + fold(dl * image),
            cross + fold(r * image),
            square + fold(image * image),
            old + fold(r * r),
        )

    zero = jnp.zeros((COLS, 128), f32)
    totals = lax.fori_loop(0, LEAVES, finish, (zero,) * 4, unroll=2)
    lane = lax.broadcasted_iota(jnp.int32, (COLS, 128), 1)
    packed = zero
    for i, total in enumerate(totals):
        packed = jnp.where(lane == i, jnp.sum(total, axis=1, keepdims=True), packed)
    packed = jnp.concatenate([packed, zero], axis=0)
    sums[...] = packed.T[:8]


def reduce_kernel(part, out, buf, send, recv):
    every = CORE + sum(RINGS, ())
    greet(every)
    value = part[...]
    await_greetings(every)
    for r, masks in enumerate((CORE,) + RINGS):
        buf[r, 0] = value
        copies = exchange(buf, r, masks, send, recv)
        for copy in copies:
            copy.start()
        for copy in copies:
            copy.wait()
        value = buf[r, 0] + buf[r, 1]
        if len(masks) == 3:
            value = value + (buf[r, 2] + buf[r, 3])
    curv, cross, square, old = value[0:1], value[1:2], value[2:3], value[3:4]
    alpha = old / curv
    new = old - 2.0 * alpha * cross + alpha * alpha * square
    beta = new / old
    row = lax.broadcasted_iota(jnp.int32, (8, 128), 0)
    out[...] = jnp.where(row == 0, alpha, jnp.where(row == 1, beta, 0.0))


def pair_lists(near_list):
    flat = near_list.reshape(-1)
    number = flat.shape[0]
    live = flat >= 0
    idx = jnp.arange(number, dtype=jnp.int32)
    place = jnp.sum(jnp.where(idx[:, None] > idx[None, :], live[None, :], False).astype(jnp.int32), axis=1)
    slot = jnp.arange(SLOTS, dtype=jnp.int32)
    hit = (place[None, :] == slot[:, None]) & live[None, :]
    code = jnp.sum(jnp.where(hit, (idx // 8)[None, :] * 128 + flat[None, :] - (31 * 128 + 64), 0), axis=1)
    code = code + (31 * 128 + 64)
    total = jnp.sum(live.astype(jnp.int32))
    return total[None], code // 128, code % 128


def shards(
    rhs, iterate, residual, direction, points, skeletons, leaf_basis, device_basis, transfer,
    node_coords, near_list, far_list,
):
    vm = pl.BlockSpec(memory_space=pltpu.VMEM)
    sm = pl.BlockSpec(memory_space=pltpu.SMEM)
    hbm = pl.BlockSpec(memory_space=pl.ANY)
    count, tg, sr = pair_lists(near_list)
    far = jnp.where(far_list < 0, 64, far_list).reshape(-1)
    wide = jax.ShapeDtypeStruct((COLS, LEAVES * LEAF), f32)
    weights = jax.ShapeDtypeStruct((LEAVES * RANK, 2 * COLS), f32)
    z0, w_own, dp, xp, wp, ptp, skp = pl.pallas_call(
        climb_kernel,
        out_shape=(
            jax.ShapeDtypeStruct((RANK, 2 * COLS), f32),
            weights,
            wide,
            wide,
            weights,
            jax.ShapeDtypeStruct(points.shape, f32),
            jax.ShapeDtypeStruct(skeletons.shape, f32),
        ),
        in_specs=[vm, vm, vm, vm, hbm, vm, vm, vm],
        out_specs=(vm,) * 7,
        scratch_shapes=[
            pltpu.VMEM((9, 64, 128), f32),
            pltpu.VMEM((6, 128, 128), f32),
            pltpu.VMEM((4, 4, 64, 128), f32),
            pltpu.SemaphoreType.DMA((6,)),
            pltpu.SemaphoreType.DMA((5,)),
            pltpu.SemaphoreType.DMA((5,)),
            pltpu.SemaphoreType.DMA((4, 3)),
            pltpu.SemaphoreType.DMA((4, 3)),
        ],
        compiler_params=pltpu.CompilerParams(
            collective_id=0, has_side_effects=True, vmem_limit_bytes=40 << 20
        ),
    )(direction, iterate, leaf_basis, device_basis, transfer, node_coords, points, skeletons)
    hd, hx, sums = pl.pallas_call(
        apply_kernel,
        out_shape=(wide, wide, jax.ShapeDtypeStruct((8, 128), f32)),
        in_specs=[sm] * 4 + [vm] * 14,
        out_specs=(vm,) * 3,
        scratch_shapes=[
            pltpu.VMEM((65, 256, 256), bf16),
            pltpu.VMEM((65, 256, 64), bf16),
            pltpu.VMEM((32, 64, 256), bf16),
            pltpu.VMEM((65, 64, 256), bf16),
            pltpu.VMEM((65, 64, 128), bf16),
            pltpu.VMEM((65, 64, 128), bf16),
            pltpu.VMEM((32, 64, 64), bf16),
            pltpu.VMEM((32, 64, 128), f32),
            pltpu.VMEM((32, 128, 256), f32),
            pltpu.VMEM((BUFS, 256, 256), bf16),
            pltpu.VMEM((BUFS, 256, 256), bf16),
        ],
        compiler_params=pltpu.CompilerParams(vmem_limit_bytes=60 << 20),
    )(
        count, tg, sr, far, direction, iterate, dp, xp, points, ptp, skeletons, skp, w_own, wp,
        leaf_basis, device_basis, z0, residual,
    )
    scalars = pl.pallas_call(
        reduce_kernel,
        out_shape=jax.ShapeDtypeStruct((8, 128), f32),
        in_specs=[vm],
        out_specs=vm,
        scratch_shapes=[
            pltpu.VMEM((4, 4, 8, 128), f32),
            pltpu.SemaphoreType.DMA((4, 3)),
            pltpu.SemaphoreType.DMA((4, 3)),
        ],
        compiler_params=pltpu.CompilerParams(collective_id=1, has_side_effects=True),
    )(sums)
    alpha = scalars[0, :COLS][:, None]
    beta = scalars[1, :COLS][:, None]
    new_iterate = iterate + alpha * direction
    new_residual = residual - alpha * hd
    new_direction = new_residual + beta * direction
    true_residual = rhs - (hx + alpha * hd)
    return (new_iterate, new_residual, new_direction, true_residual)


def solution(mesh):
    wide = P(None, ("leaf", "sub"))
    rows = P(("leaf", "sub"), None)
    return jax.shard_map(
        shards,
        mesh=mesh,
        in_specs=(wide,) * 8 + (P(), P(), rows, rows),
        out_specs=(wide,) * 4,
        check_vma=False,
    )
```

time: 855 us -> 130 us (0.15); the launches traced: 844 us -> 130 us
  matrix products: 484 us -> 0 us
  blocking collectives: 128 us -> 0 us
  local copies, waits for them, and re-layouts: 129 us -> 17.4 us
  Pallas kernels: 0 us -> 100 us
  other arithmetic: 50.7 us -> 11 us
  waiting for transfers between devices: 25.1 us -> 0 us
  starting transfers between devices: 22.9 us -> 0 us
    dot_general x85 -> x0, matrix products: 484 us -> none  [the longest x16 218 us: near_block(): terms = jnp.einsum('nbq,bqp->bnp', source_vec, kernel, precision=highest)]
    psum x2 -> x0, blocking collectives: 128 us -> none  [the longest x1 64.5 us: shards(): lax.psum(jnp.sum(new_residual * new_residual, axis=1), ('leaf', 'sub'))]
    pallas_call x0 -> x3, Pallas kernels: none -> 100 us  [the longest x1 52.1 us: shards(): pl.pallas_call(apply_kernel, out_shape=(wide, wide, jax.ShapeDtypeStruct(...]
    gather x52 -> x0, local copies, waits for them, and re-layouts: 76.5 us -> none  [the longest x16 45.9 us: near_block(): source_vec = jnp.take(vector_tab, sources, axis=1)]
    reduce_sum x40 -> x3, other arithmetic: 33.4 us -> 1.63 us  [the longest x1 1.39 us: pair_lists(): total = jnp.sum(live.astype(jnp.int32))]
    ppermute x20 -> x0, waiting for transfers between devices: 25.1 us -> none  [from_partner(): lax.ppermute(value, axis, [(i, i ^ 1 << apart) for i in range(lax.axis_si...]
    ppermute x20 -> x0, starting transfers between devices: 22.9 us -> none  [from_partner(): lax.ppermute(value, axis, [(i, i ^ 1 << apart) for i in range(lax.axis_si...]
    another operation x3 -> x0, local copies, waits for them, and re-layouts: 15.8 us -> none
  transfers between devices with their start and end apart: 20 -> 0, of which waited for: 10 -> 0; matrix products, arithmetic and copies ran while one was open for 15% -> 0% of each run, Pallas kernels for 0% -> 0%
where the time goes in v1:
time: 130 us
  Pallas kernels  100 us (77%)
  local copies, waits for them, and re-layouts  17.4 us (13%)
  other arithmetic  11 us (8%)
    pallas_call x1, Pallas kernels, shards(): pl.pallas_call(apply_kernel, out_shape=(wide, wide, jax.ShapeDtypeStruct(...  52.1 us
    pallas_call x1, Pallas kernels, shards(): pl.pallas_call(climb_kernel, out_shape=(jax.ShapeDtypeStruct((RANK, 2 * C...  30.6 us
    pallas_call x1, Pallas kernels, shards(): pl.pallas_call(reduce_kernel, out_shape=jax.ShapeDtypeStruct((8, 128), f3...  17.7 us
    unnamed x31, local copies, waits for them, and re-layouts  15.8 us
    add x1, other arithmetic, shards(): new_direction = new_residual + beta * direction  8 us

profile of v1, /device:TPU:0, one launch (start us, length us, event | category | flops | bytes accessed | tf_op | source)
XLA Modules:
  0.0 129.5 jit_solution(3206460617351631465)
XLA Ops:
  0.6 1.4 %convert_reduce_fusion.1 = s32[]{:T(128)} fusion(s32[32,8]{0,1:T(8,128)} %param.22), kind=kLoop, calls=%fused_computation.11 | loop fusion | flops 767 | bytes 1028 | tf_op jit(solution)/shard_map/reduce_sum | solution.py:360
  2.0 0.7 compare_select_fusion
  2.7 0.1 copy.19
  2.8 0.7 reshape.47.far
  3.5 0.8 copy.18
  4.2 0.1 reshape.46
  4.3 0.1 convert_reduce_fusion
  4.5 0.1 select_reduce_fusion
  4.6 0.6 and_select_fusion
  5.2 0.0 copy-start
  5.2 1.6 %copy-done = f32[64,8192]{1,0:T(8,128)S(1)} copy-done((f32[64,8192]{1,0:T(8,128)S(1)}, f32[64,8192]{1,0:T(8,128)}, u32[]{:S(2)}) %copy-start) | copy-done | bytes 2097176
  6.8 0.0 copy-start.2
  6.8 1.6 %copy-done.2 = f32[64,8192]{1,0:T(8,128)S(1)} copy-done((f32[64,8192]{1,0:T(8,128)S(1)}, f32[64,8192]{1,0:T(8,128)}, u32[]{:S(2)}) %copy-start.2) | copy-done | bytes 2097176
  8.4 1.6 %copy-done.3 = f32[64,8192]{1,0:T(8,128)S(1)} copy-done((f32[64,8192]{1,0:T(8,128)S(1)}, f32[64,8192]{1,0:T(8,128)}, u32[]{:S(2)}) %copy-start.3) | copy-done | bytes 2097176
  10.0 1.0 copy-done.6
  11.0 0.9 copy-done.7
  12.0 0.8 copy-done.11
  12.8 0.9 copy-done.12
  13.8 30.6 %shard_map.147 = (f32[64,128]{1,0:T(8,128)S(1)}, f32[2048,128]{1,0:T(8,128)S(1)}, f32[64,8192]{1,0:T(8,128)S(1)}, f32[64,8192]{1,0:T(8,128)S(1)}, f32[2048,128]{...) custom-call(f32[64,8192]{1,0:T(8,128)S(1)} %copy-done, f32[64,8192]{1,0:T(8,128)S(1)} %copy-done.2, ...), custom_call_target="tpu_custom_call" | custom-call | tf_op jit(solution)/shard_map/pallas_call | solution.py:375
  44.4 0.0 copy-start.4
  44.4 1.3 %copy-done.4 = f32[64,8192]{1,0:T(8,128)} copy-done((f32[64,8192]{1,0:T(8,128)}, f32[64,8192]{1,0:T(8,128)S(1)}, u32[]{:S(2)}) %copy-start.4) | copy-done | bytes 2097176
  45.7 1.3 %copy-done.5 = f32[64,8192]{1,0:T(8,128)} copy-done((f32[64,8192]{1,0:T(8,128)}, f32[64,8192]{1,0:T(8,128)S(1)}, u32[]{:S(2)}) %copy-start.5) | copy-done | bytes 2097176
  47.0 1.0 copy-done.8
  48.0 1.0 copy-done.9
  49.0 0.7 copy-done.10
  49.7 0.6 copy-done.13
  50.3 0.6 copy-done.14
  50.9 52.1 %shard_map.148 = (f32[64,8192]{1,0:T(8,128)}, f32[64,8192]{1,0:T(8,128)}, f32[8,128]{1,0:T(8,128)}) custom-call(s32[1]{0:T(128)} %bitcast.count, s32[200]{0:T(256)} %get-tuple-element.31.tg, s32[200]{0:T(256)} %get-tuple-element.30.sr, s32[256]{0:T(256)} %reshape.47.far, f32[64,8192]{1,0:T(8,128)} %d.3, f32[64,8192]{1,0:T(8,128)} %x.3, ...), custom_call_target="tpu_custom_call" | custom-call | tf_op jit(solution)/shard_map/pallas_call | solution.py:402
  103.0 17.7 %shard_map.149 = f32[8,128]{1,0:T(8,128)} custom-call(f32[8,128]{1,0:T(8,128)} %get-tuple-element.21.part), custom_call_target="tpu_custom_call" | custom-call | tf_op jit(solution)/shard_map/pallas_call | solution.py:425
  120.8 0.8 slice_bitcast_fusion
  121.5 0.0 copy-done.1
  121.5 8.0 %multiply_add_fusion = (f32[64,8192]{1,0:T(8,128)}, f32[64,8192]{1,0:T(8,128)}, f32[64,8192]{1,0:T(8,128)}, f32[64,8192]{1,0:T(8,128)}) fusion(f32[64,8192]{1,0:T(8,128)S(1)} %copy-done.1, f32[64]{0:T(128)S(1)} %get-tuple-element.28, f32[64,8192]{1,0:T(8,128)} %res.1, f32[64,8192]{1,0:T(8,128)} %get-tuple-element.22, f32[64]{0:T(128)S(1)} %get-tuple-element.29, ...), kind=kLoop, calls=%fused_computation.1 | loop fusion | flops 4194304 | bytes 20972032 | tf_op jit(solution)/shard_map/add | solution.py:441
  (14 shorter events, 0.0 us)
Async XLA Ops:
  5.2 1.6 %copy-start = (f32[64,8192]{1,0:T(8,128)S(1)}, f32[64,8192]{1,0:T(8,128)}, u32[]{:S(2)}) copy-start(f32[64,8192]{1,0:T(8,128)} %d.3) | copy-start | bytes 6291460
  6.8 1.6 %copy-start.2 = (f32[64,8192]{1,0:T(8,128)S(1)}, f32[64,8192]{1,0:T(8,128)}, u32[]{:S(2)}) copy-start(f32[64,8192]{1,0:T(8,128)} %x.3) | copy-start | bytes 6291460
  8.4 1.6 %copy-start.3 = (f32[64,8192]{1,0:T(8,128)S(1)}, f32[64,8192]{1,0:T(8,128)}, u32[]{:S(2)}) copy-start(f32[64,8192]{1,0:T(8,128)} %lb.3) | copy-start | bytes 6291460
  10.0 1.0 copy-start.6
  11.0 0.9 copy-start.7
  12.0 0.8 copy-start.11
  12.8 0.9 copy-start.12
  44.4 1.3 %copy-start.4 = (f32[64,8192]{1,0:T(8,128)}, f32[64,8192]{1,0:T(8,128)S(1)}, u32[]{:S(2)}) copy-start(f32[64,8192]{1,0:T(8,128)S(1)} %get-tuple-element.14.dp) | copy-start | bytes 6291460
  45.7 1.3 %copy-start.5 = (f32[64,8192]{1,0:T(8,128)}, f32[64,8192]{1,0:T(8,128)S(1)}, u32[]{:S(2)}) copy-start(f32[64,8192]{1,0:T(8,128)S(1)} %get-tuple-element.15.xp) | copy-start | bytes 6291460
  47.0 1.0 copy-start.8
  48.0 1.0 copy-start.9
  49.0 0.7 copy-start.10
  49.7 0.6 copy-start.13
  50.3 0.6 copy-start.14
  50.9 70.6 %copy-start.1 = (f32[64,8192]{1,0:T(8,128)S(1)}, f32[64,8192]{1,0:T(8,128)}, u32[]{:S(2)}) copy-start(f32[64,8192]{1,0:T(8,128)} %d.3) | copy-start | bytes 6291460

commit v2 on v1

v2 whole, which is shorter than its diff:
```python
import functools
import math

import jax
import jax.numpy as jnp
from jax import lax
from jax.experimental import pallas as pl
from jax.experimental.pallas import tpu as pltpu
from jax.sharding import PartitionSpec as P

MESH = pl.DeviceIdType.MESH
f32, bf16 = jnp.float32, jnp.bfloat16
noise_level = 1.0
amplitude = 0.1
length_scale = 1.0
LN2 = math.log(2.0)
COORD = math.sqrt(3.0) / length_scale / LN2
LEAVES, LEAF, RANK, COLS = 32, 256, 64, 64
SLOTS, BUFS, AHEAD = 200, 8, 4
ENDS, FARS = SLOTS, SLOTS + LEAVES
STEPS, CHUNKS = 24, 4
RING_AT, DOWN_AT = (3, 7, 11), 15
VMEM_LIMIT = 63 << 20
CORE = (1,)
RINGS = ((2, 4, 6), (8, 16, 24), (32, 64, 96))


def dot(a, b):
    return lax.dot_general(a, b, (((1,), (0,)), ((), ())), preferred_element_type=f32)


def dot_nt(a, b):
    return lax.dot_general(a, b, (((1,), (1,)), ((), ())), preferred_element_type=f32)


def split(a):
    hi = a.astype(bf16)
    return hi, (a - hi.astype(f32)).astype(bf16)


def dot3(a, b):
    ah, al = split(a)
    bh, bl = split(b)
    return dot(ah, bh) + (dot(ah, bl) + dot(al, bh))


def kern(u):
    t = jnp.maximum(u, 1e-12)
    s = t * lax.rsqrt(t)
    return (amplitude + (amplitude * LN2) * s) * jnp.exp2(-s)


def pieces(a):
    one = a.astype(bf16).astype(f32)
    rest = a - one
    two = rest.astype(bf16).astype(f32)
    three = (rest - two).astype(bf16).astype(f32)
    return one, two, three


def features(coords):
    a = coords * COORD
    a1, a2, a3 = pieces(a)
    n1, n2, n3 = pieces(jnp.sum(a * a, axis=0, keepdims=True))
    row = lax.broadcasted_iota(jnp.int32, a.shape, 0)
    norm = jnp.where((row == 0) | (row == 3), n1, jnp.where((row == 1) | (row == 4), n2, n3))
    zero = jnp.zeros_like(a)
    src_norm = jnp.where(row < 3, norm, jnp.where(row < 6, 1.0, 0.0))
    tgt_norm = jnp.where(row < 3, 1.0, jnp.where(row < 6, norm, 0.0))
    s1, s2, s3 = -2.0 * a1, -2.0 * a2, -2.0 * a3
    source = jnp.concatenate([s1, s1, s2, s2, s1, s3, src_norm, zero], axis=0)
    target = jnp.concatenate([a1, a2, a1, a2, a3, a1, tgt_norm, zero], axis=0)
    return source, target


def tree_position():
    return lax.axis_index("sub") * 32 + lax.axis_index("leaf")


def device_at(q):
    return (lax.rem(q, 32), lax.div(q, 32))


def greet(masks):
    q = tree_position()
    barrier = pltpu.get_barrier_semaphore()
    for mask in masks:
        pl.semaphore_signal(barrier, inc=1, device_id=device_at(q ^ mask), device_id_type=MESH)


def await_greetings(masks):
    pl.semaphore_wait(pltpu.get_barrier_semaphore(), len(masks))


def exchange(buf, number, masks, send, recv):
    q = tree_position()
    return [
        pltpu.make_async_remote_copy(
            buf.at[number, 0],
            buf.at[number, i + 1],
            send.at[number, i],
            recv.at[number, i],
            device_id=device_at(q ^ mask),
            device_id_type=MESH,
        )
        for i, mask in enumerate(masks)
    ]


def step_kernel(
    meta, d_in, x_in, lb_in, db_in, transfer, nc_in, pts_in, sk_in, res_in,
    hd_out, hx_out, scalars,
    d, x, lb, db, nc, pts, sk, dp, xp, ptp, skp, w_own, wp,
    mats, kmask, buf, stk, z0, vt, fs, ft, wt, fte, fto, fsk, zl, zt, terms, kh, kl, tot, abuf,
    in_sem, mat_sem, far_send, far_recv, send, recv, asend, arecv, out_sem,
):
    q = tree_position()
    every = CORE + sum(RINGS, ())
    greet(every)
    chunk = LEAVES * LEAF // CHUNKS
    loads = [
        pltpu.make_async_copy(a, b, in_sem.at[i])
        for i, (a, b) in enumerate(((pts_in, pts), (sk_in, sk), (nc_in, nc), (db_in, db)))
    ]
    for load in loads[:1]:
        load.start()
    parts = []
    for c in range(CHUNKS):
        at = pl.ds(c * chunk, chunk)
        parts.append([
            pltpu.make_async_copy(a.at[:, at], b.at[:, at], in_sem.at[5 + 3 * c + i])
            for i, (a, b) in enumerate(((d_in, d), (x_in, x), (lb_in, lb)))
        ])
        for load in parts[-1]:
            load.start()
        if c == 0:
            for load in loads[1:]:
                load.start()
    spots = []
    for c in range(1, 7):
        base = 128 - 2 * (128 >> c)
        node = lax.shift_right_logical(q, c)
        if c % 2:
            spots.append((base + node, 1, (c - 1) // 2 * 3))
        else:
            spots.append((base + (node & -2), 2, (c - 2) // 2 * 3 + 1))
    mat_loads = [
        pltpu.make_async_copy(transfer.at[pl.ds(at, n)], mats.at[pl.ds(slot, n)], mat_sem.at[i])
        for i, (at, n, slot) in enumerate(spots)
    ]
    for load in mat_loads:
        load.start()

    def lanes(l, width):
        return pl.ds(pl.multiple_of(l * width, width), width)

    loads[0].wait()

    def own_points(l, carry):
        source, target = features(pts[:, lanes(l, LEAF)])
        fs[l] = source.T.astype(bf16)
        ft[l] = target.astype(bf16)
        return carry

    lax.fori_loop(0, LEAVES, own_points, 0, unroll=4)
    await_greetings(every)
    partner = device_at(q ^ 1)
    bulk = [
        pltpu.make_async_remote_copy(
            a, b, far_send.at[i], far_recv.at[i], device_id=partner, device_id_type=MESH
        )
        for i, (a, b) in enumerate(
            ((pts_in, ptp), (d_in, dp), (x_in, xp), (sk_in, skp), (w_own, wp))
        )
    ]
    for copy in bulk[:4]:
        copy.start()

    def leaf(l, carry):
        at = lanes(l, LEAF)
        vh, vl = split(jnp.concatenate([d[:, at], x[:, at]], axis=0))
        vt[l] = jnp.concatenate([vh, vl], axis=0)
        bh, bl = split(lb[:, at])
        both = dot_nt(jnp.concatenate([bh, bl], axis=0), vh)
        w_own[lanes(l, RANK), :] = both[:RANK] + both[RANK:] + dot_nt(bh, vl)
        return carry

    for c in range(CHUNKS):
        for load in parts[c]:
            load.wait()
        lax.fori_loop(c * LEAVES // CHUNKS, (c + 1) * LEAVES // CHUNKS, leaf, 0, unroll=4)
    bulk[4].start()
    for load in loads[1:]:
        load.wait()
    buf[0, 0] = dot3(db[...], w_own[...])
    for copy in exchange(buf, 0, CORE, send, recv):
        copy.start()

    row = lax.broadcasted_iota(jnp.int32, (128, 128), 0)
    col = lax.broadcasted_iota(jnp.int32, (128, 128), 1)
    for c in range(1, 7):
        start = 64 * (128 - 2 * (128 >> c)) + 128 * lax.shift_right_logical(q, c + 1)
        source, target = features(nc[:, pl.ds(pl.multiple_of(start, 128), 128)])
        full = kern(dot(source.T.astype(bf16), target.astype(bf16)))
        kmask[c - 1] = jnp.where((row < 64) == (col < 64), 0.0, full)
    for load in mat_loads:
        load.wait()

    def skel_tables(side, ss, ww):
        low = lax.broadcasted_iota(jnp.int32, (64, 128), 1) < 64

        def one_pair(m, carry):
            source, target = features(ss[:, lanes(m, 128)])
            turned = pltpu.roll(target, 64, 1)
            one = side * LEAVES + 2 * m
            fte[one] = jnp.where(low, target, 0.0).astype(bf16)
            fto[one] = jnp.where(low, 0.0, turned).astype(bf16)
            fte[one + 1] = jnp.where(low, turned, 0.0).astype(bf16)
            fto[one + 1] = jnp.where(low, 0.0, target).astype(bf16)
            for i in range(2):
                hi, lo = split(ww[pl.ds(pl.multiple_of(m * 128 + i * 64, 64), 64), :])
                wt[one + i] = jnp.concatenate([hi, lo], axis=1)
            if side == 0:
                flipped = source.T.astype(bf16)
                fsk[2 * m] = flipped[:64]
                fsk[2 * m + 1] = flipped[64:]
            return carry

        lax.fori_loop(0, LEAVES // 2, one_pair, 0, unroll=4)

    skel_tables(0, sk, w_own)
    vt[2 * LEAVES] = jnp.zeros((4 * COLS, LEAF), bf16)
    fs[2 * LEAVES] = jnp.zeros((LEAF, 64), bf16)
    wt[2 * LEAVES] = jnp.zeros((RANK, 4 * COLS), bf16)
    fte[2 * LEAVES] = jnp.zeros((64, 128), bf16)
    fto[2 * LEAVES] = jnp.zeros((64, 128), bf16)
    terms[0] = jnp.zeros((2 * COLS, LEAF), f32)
    zero = jnp.zeros((COLS, 128), f32)
    for i in range(4):
        tot[i] = zero

    def pair(number, a, b):
        return jnp.concatenate([buf[number, a ^ (2 * b)], buf[number, a ^ (2 * b + 1)]], axis=0)

    def half(value, c):
        return jnp.where((lax.shift_right_logical(q, c) & 1) == 0, value[:64], value[64:])

    def climb_core():
        for copy in exchange(buf, 0, CORE, send, recv):
            copy.wait()
        h = q & 1
        bottom = jnp.concatenate([buf[0, h], buf[0, h ^ 1]], axis=0)
        buf[1, 0] = dot3(mats[0], bottom)
        for copy in exchange(buf, 1, RINGS[0], send, recv):
            copy.start()

    def climb_ring(r):
        for copy in exchange(buf, r + 1, RINGS[r], send, recv):
            copy.wait()
        a = lax.shift_right_logical(q, 2 * r + 1) & 3
        e = a & 2
        stk[2 * r] = jnp.concatenate([buf[r + 1, a ^ e], buf[r + 1, a ^ (e + 1)]], axis=0)
        upper = jnp.concatenate(
            [dot3(mats[3 * r + 1 + b], pair(r + 1, a, b)) for b in range(2)], axis=0
        )
        stk[2 * r + 1] = upper
        if r < 2:
            buf[r + 2, 0] = dot3(mats[3 * r + 3], upper)
            for copy in exchange(buf, r + 2, RINGS[r + 1], send, recv):
                copy.start()

    def descend():
        down = half(dot3(kmask[5], stk[5]), 6)
        for c in range(6, 0, -1):
            if c % 2:
                matrix = mats[(c - 1) // 2 * 3]
            else:
                matrix = mats[(c - 2) // 2 * 3 + 1 + (lax.shift_right_logical(q, c) & 1)]
            children = dot3(matrix.T, down)
            if c > 1:
                children = children + dot3(kmask[c - 2], stk[c - 2])
            down = half(children, c - 1)
        z0[...] = down

    climb_core()

    for copy in bulk[:3]:
        copy.wait()

    def partner_points(l, carry):
        at = lanes(l, LEAF)
        source, target = features(ptp[:, at])
        fs[LEAVES + l] = source.T.astype(bf16)
        hi, lo = split(jnp.concatenate([dp[:, at], xp[:, at]], axis=0))
        vt[LEAVES + l] = jnp.concatenate([hi, lo], axis=0)
        return carry

    lax.fori_loop(0, LEAVES, partner_points, 0, unroll=4)
    res_load = pltpu.make_async_copy(res_in, dp, in_sem.at[4])
    res_load.start()

    def tile(k, b):
        code = meta[k]
        hi, lo = split(kern(dot(fs[code & 127], ft[lax.shift_right_logical(code, 7) & 31])))
        kh[b] = hi
        kl[b] = lo

    def multiply(k, b):
        code = meta[k]
        v = vt[code & 127]
        keep = lax.shift_right_logical(code, 12).astype(f32)
        both = dot(v, kh[b])
        terms[k + 1] = terms[k] * keep + (
            both[: 2 * COLS] + both[2 * COLS :] + dot(v[: 2 * COLS], kl[b])
        )

    for j in range(AHEAD):
        tile(j, j)

    def near(i, carry):
        for r in range(3):
            @pl.when(i == RING_AT[r])
            def _():
                climb_ring(r)

        @pl.when(i == DOWN_AT)
        def _():
            descend()

        for j in range(BUFS):
            k = i * BUFS + j
            multiply(k, j)
            tile(k + AHEAD, (j + AHEAD) % BUFS)
        return carry

    lax.fori_loop(0, STEPS, near, 0)

    for copy in bulk[3:]:
        copy.wait()
    skel_tables(1, skp, wp)

    def down_to_leaves(m, carry):
        dh, dl = split(db[:, lanes(m, 128)].T)
        zh, zlo = split(z0[...])
        part = dot(dh, zh) + (dot(dh, zlo) + dot(dl, zh))
        zl[2 * m] = part[:64]
        zl[2 * m + 1] = part[64:]
        return carry

    lax.fori_loop(0, LEAVES // 2, down_to_leaves, 0, unroll=4)

    def farther(l, carry):
        across = []
        rows = []
        for j in range(4):
            one, two = meta[FARS + l * 8 + 2 * j], meta[FARS + l * 8 + 2 * j + 1]
            across.append(fte[one] + fto[two])
            rows += [wt[one], wt[two]]
        hi, lo = split(kern(dot(fsk[l], jnp.concatenate(across, axis=1))))
        got = dot(jnp.concatenate([hi, lo], axis=0), jnp.concatenate(rows, axis=0))
        zl[l] += got[:64, :128] + got[:64, 128:] + got[64:, :128]
        return carry

    lax.fori_loop(0, LEAVES, farther, 0, unroll=4)

    def turn(l, carry):
        z = zl[l]
        zh = z.astype(bf16).astype(f32)
        zt[l] = jnp.concatenate([zh, z - zh], axis=0).T.astype(bf16)
        return carry

    lax.fori_loop(0, LEAVES, turn, 0, unroll=8)
    res_load.wait()

    def fold(value):
        return value[:, :128] + value[:, 128:]

    def finish(l, carry):
        at = lanes(l, LEAF)
        bh, bl = split(lb[:, at])
        zz = zt[l]
        out = terms[meta[ENDS + l]] + (
            dot(zz, jnp.concatenate([bh, bh], axis=0)) + dot(zz[:, :64], bl)
        )
        dl = d[:, at]
        r = dp[:, at]
        image = noise_level * dl + out[:COLS]
        tot[0] += fold(dl * image)
        tot[1] += fold(r * image)
        tot[2] += fold(image * image)
        tot[3] += fold(r * r)
        d[:, at] = image
        x[:, at] = noise_level * x[:, at] + out[COLS:]
        return carry

    lax.fori_loop(0, LEAVES, finish, 0, unroll=4)
    outs = [
        pltpu.make_async_copy(a, b, out_sem.at[i])
        for i, (a, b) in enumerate(((d, hd_out), (x, hx_out)))
    ]
    for out in outs:
        out.start()

    lane = lax.broadcasted_iota(jnp.int32, (COLS, 128), 1)
    packed = zero
    for i in range(4):
        packed = jnp.where(lane == i, jnp.sum(tot[i], axis=1, keepdims=True), packed)
    value = jnp.concatenate([packed, zero], axis=0).T[:8]
    for r, masks in enumerate((CORE,) + RINGS):
        abuf[r, 0] = value
        copies = exchange(abuf, r, masks, asend, arecv)
        for copy in copies:
            copy.start()
        for copy in copies:
            copy.wait()
        value = abuf[r, 0] + abuf[r, 1]
        if len(masks) == 3:
            value = value + (abuf[r, 2] + abuf[r, 3])
    curv, cross, square, old = value[0:1], value[1:2], value[2:3], value[3:4]
    alpha = old / curv
    new = old - 2.0 * alpha * cross + alpha * alpha * square
    beta = new / old
    eight = lax.broadcasted_iota(jnp.int32, (8, 128), 0)
    scalars[...] = jnp.where(eight == 0, alpha, jnp.where(eight == 1, beta, 0.0))
    for out in outs:
        out.wait()


def lists(near_list, far_list):
    counts = jnp.sum((near_list >= 0).astype(jnp.int32), axis=1)
    leaf = jnp.arange(LEAVES, dtype=jnp.int32)
    before = jnp.sum(jnp.where(leaf[:, None] > leaf[None, :], counts[None, :], 0), axis=1)
    place = before[:, None] + jnp.arange(8, dtype=jnp.int32)[None, :]
    first = jnp.arange(8, dtype=jnp.int32)[None, :] == 0
    code = near_list + leaf[:, None] * 128 + jnp.where(first, 0, 4096)
    nothing = 64 + 31 * 128 + 4096
    slot = jnp.arange(SLOTS, dtype=jnp.int32)[:, None, None]
    hit = (place[None] == slot) & (near_list >= 0)[None]
    pairs = jnp.sum(jnp.where(hit, code[None] - nothing, 0), axis=(1, 2)) + nothing
    far = jnp.where(far_list < 0, 64, far_list).reshape(-1)
    return jnp.concatenate([pairs, before + counts, far])


def shards(
    rhs, iterate, residual, direction, points, skeletons, leaf_basis, device_basis, transfer,
    node_coords, near_list, far_list,
):
    vm = pl.BlockSpec(memory_space=pltpu.VMEM)
    sm = pl.BlockSpec(memory_space=pltpu.SMEM)
    hbm = pl.BlockSpec(memory_space=pl.ANY)
    wide = jax.ShapeDtypeStruct((COLS, LEAVES * LEAF), f32)
    big = pltpu.VMEM((COLS, LEAVES * LEAF), f32)
    weights = pltpu.VMEM((LEAVES * RANK, 2 * COLS), f32)
    point_buf = pltpu.VMEM(points.shape, f32)
    skel_buf = pltpu.VMEM(skeletons.shape, f32)
    dma = pltpu.SemaphoreType.DMA
    hd, hx, scalars = pl.pallas_call(
        step_kernel,
        out_shape=(wide, wide, jax.ShapeDtypeStruct((8, 128), f32)),
        in_specs=[sm] + [hbm] * 9,
        out_specs=(hbm, hbm, vm),
        scratch_shapes=[
            big, big, big,
            pltpu.VMEM(device_basis.shape, f32),
            pltpu.VMEM(node_coords.shape, f32),
            point_buf, skel_buf,
            big, big, point_buf, skel_buf, weights, weights,
            pltpu.VMEM((9, 64, 128), f32),
            pltpu.VMEM((6, 128, 128), f32),
            pltpu.VMEM((4, 4, 64, 128), f32),
            pltpu.VMEM((6, 128, 128), f32),
            pltpu.VMEM((64, 128), f32),
            pltpu.VMEM((65, 256, 256), bf16),
            pltpu.VMEM((65, 256, 64), bf16),
            pltpu.VMEM((32, 64, 256), bf16),
            pltpu.VMEM((65, 64, 256), bf16),
            pltpu.VMEM((65, 64, 128), bf16),
            pltpu.VMEM((65, 64, 128), bf16),
            pltpu.VMEM((32, 64, 64), bf16),
            pltpu.VMEM((32, 64, 128), f32),
            pltpu.VMEM((32, 128, 128), bf16),
            pltpu.VMEM((STEPS * BUFS + 1, 128, 256), f32),
            pltpu.VMEM((BUFS, 256, 256), bf16),
            pltpu.VMEM((BUFS, 256, 256), bf16),
            pltpu.VMEM((4, 64, 128), f32),
            pltpu.VMEM((4, 4, 8, 128), f32),
            dma((5 + 3 * CHUNKS,)), dma((6,)), dma((5,)), dma((5,)),
            dma((4, 3)), dma((4, 3)), dma((4, 3)), dma((4, 3)), dma((2,)),
        ],
        compiler_params=pltpu.CompilerParams(
            collective_id=0, has_side_effects=True, vmem_limit_bytes=VMEM_LIMIT
        ),
    )(
        lists(near_list, far_list), direction, iterate, leaf_basis, device_basis, transfer,
        node_coords, points, skeletons, residual,
    )
    alpha = scalars[0, :COLS][:, None]
    beta = scalars[1, :COLS][:, None]
    new_iterate = iterate + alpha * direction
    new_residual = residual - alpha * hd
    new_direction = new_residual + beta * direction
    true_residual = rhs - (hx + alpha * hd)
    return (new_iterate, new_residual, new_direction, true_residual)


def solution(mesh):
    wide = P(None, ("leaf", "sub"))
    rows = P(("leaf", "sub"), None)
    return jax.shard_map(
        shards,
        mesh=mesh,
        in_specs=(wide,) * 8 + (P(), P(), rows, rows),
        out_specs=(wide,) * 4,
        check_vma=False,
    )
```

time: 130 us -> 85 us (0.65)
  Pallas kernels: 100 us -> 71.9 us
  local copies, waits for them, and re-layouts: 17.4 us -> 1.1 us
    pallas_call x3 -> x1, Pallas kernels: 100 us -> 71.9 us  [shards(): pl.pallas_call(step_kernel, out_shape=(wide, wide, jax.ShapeDtypeStruct((...]
    unnamed x31 -> x0, local copies, waits for them, and re-layouts: 15.8 us -> none
where the time goes in v2:
time: 85 us; the launch traced here: 84.8 us
  Pallas kernels  71.9 us (85%)
  other arithmetic  11.1 us (13%)
  local copies, waits for them, and re-layouts  1.1 us (1%)
    pallas_call x1, Pallas kernels, shards(): pl.pallas_call(step_kernel, out_shape=(wide, wide, jax.ShapeDtypeStruct((...  71.9 us
    add x1, other arithmetic, shards(): new_direction = new_residual + beta * direction  8.65 us

profile of v2, /device:TPU:0, one launch (start us, length us, event | category | flops | bytes accessed | tf_op | source)
XLA Modules:
  0.0 84.8 jit_solution(338488404485441654)
XLA Ops:
  0.7 0.7 compare_select_fusion
  1.3 0.8 convert_reduce_fusion
  2.1 0.1 select_reduce_fusion.1
  2.2 0.1 copy.21
  2.3 0.1 copy.23
  2.4 0.1 reshape.47
  2.5 0.1 iota_add_fusion
  2.6 0.1 copy.22
  2.6 0.2 select_reduce_fusion
  2.8 0.7 pad_add_fusion.meta
  3.5 71.9 %shard_map.147 = (f32[64,8192]{1,0:T(8,128)}, f32[64,8192]{1,0:T(8,128)}, f32[8,128]{1,0:T(8,128)}) custom-call(s32[488]{0:T(512)} %pad_add_fusion.meta, f32[64,8192]{1,0:T(8,128)} %d_in.1, f32[64,8192]{1,0:T(8,128)} %x_in.1, f32[64,8192]{1,0:T(8,128)} %lb_in.1, f32[64,2048]{1,0:T(8,128)} %db_in.1, f32[126,64,128]{2,1,0:T(8,128)} %transfer.1, ...), custom_call_target="tpu_custom_call" | custom-call | tf_op jit(solution)/shard_map/pallas_call | solution.py:457
  75.4 0.8 slice_bitcast_fusion
  76.2 8.6 %multiply_add_fusion = (f32[64,8192]{1,0:T(8,128)}, f32[64,8192]{1,0:T(8,128)}, f32[64,8192]{1,0:T(8,128)}, f32[64,8192]{1,0:T(8,128)}) fusion(f32[64,8192]{1,0:T(8,128)} %d_in.1, f32[64]{0:T(128)S(1)} %get-tuple-element.16, f32[64,8192]{1,0:T(8,128)} %res_in.1, f32[64,8192]{1,0:T(8,128)} %get-tuple-element.8, f32[64]{0:T(128)S(1)} %get-tuple-element.17, ...), kind=kLoop, calls=%fused_computation.1 | loop fusion | flops 4194304 | bytes 20972032 | tf_op jit(solution)/shard_map/add | solution.py:501
  (4 shorter events, 0.0 us)

commit v3 on v2

--- a/solution.py
+++ b/solution.py
@@ -19,7 +19,8 @@
 SLOTS, BUFS, AHEAD = 200, 8, 4
 ENDS, FARS = SLOTS, SLOTS + LEAVES
 STEPS, CHUNKS = 24, 4
-RING_AT, DOWN_AT = (3, 7, 11), 15
+RING_AT, DOWN_AT = (5, 9, 13), 17
+ALONE, UPDATE = 3, 2048
 VMEM_LIMIT = 63 << 20
 CORE = (1,)
 RINGS = ((2, 4, 6), (8, 16, 24), (32, 64, 96))
@@ -108,11 +109,11 @@
 
 
 def step_kernel(
-    meta, d_in, x_in, lb_in, db_in, transfer, nc_in, pts_in, sk_in, res_in,
-    hd_out, hx_out, scalars,
+    meta, d_in, x_in, lb_in, db_in, transfer, nc_in, pts_in, sk_in, res_in, rhs_in,
+    hd_out, gap_out, scalars,
     d, x, lb, db, nc, pts, sk, dp, xp, ptp, skp, w_own, wp,
     mats, kmask, buf, stk, z0, vt, fs, ft, wt, fte, fto, fsk, zl, zt, terms, kh, kl, tot, abuf,
-    in_sem, mat_sem, far_send, far_recv, send, recv, asend, arecv, out_sem,
+    in_sem, mat_sem, far_send, far_recv, send, recv, asend, arecv, out_sem, late_sem,
 ):
     q = tree_position()
     every = CORE + sum(RINGS, ())
@@ -154,15 +155,6 @@
     def lanes(l, width):
         return pl.ds(pl.multiple_of(l * width, width), width)
 
-    loads[0].wait()
-
-    def own_points(l, carry):
-        source, target = features(pts[:, lanes(l, LEAF)])
-        fs[l] = source.T.astype(bf16)
-        ft[l] = target.astype(bf16)
-        return carry
-
-    lax.fori_loop(0, LEAVES, own_points, 0, unroll=4)
     await_greetings(every)
     partner = device_at(q ^ 1)
     bulk = [
@@ -175,6 +167,16 @@
     ]
     for copy in bulk[:4]:
         copy.start()
+
+    loads[0].wait()
+
+    def own_points(l, carry):
+        source, target = features(pts[:, lanes(l, LEAF)])
+        fs[l] = source.T.astype(bf16)
+        ft[l] = target.astype(bf16)
+        return carry
+
+    lax.fori_loop(0, LEAVES, own_points, 0, unroll=4)
 
     def leaf(l, carry):
         at = lanes(l, LEAF)
@@ -282,23 +284,6 @@
             down = half(children, c - 1)
         z0[...] = down
 
-    climb_core()
-
-    for copy in bulk[:3]:
-        copy.wait()
-
-    def partner_points(l, carry):
-        at = lanes(l, LEAF)
-        source, target = features(ptp[:, at])
-        fs[LEAVES + l] = source.T.astype(bf16)
-        hi, lo = split(jnp.concatenate([dp[:, at], xp[:, at]], axis=0))
-        vt[LEAVES + l] = jnp.concatenate([hi, lo], axis=0)
-        return carry
-
-    lax.fori_loop(0, LEAVES, partner_points, 0, unroll=4)
-    res_load = pltpu.make_async_copy(res_in, dp, in_sem.at[4])
-    res_load.start()
-
     def tile(k, b):
         code = meta[k]
         hi, lo = split(kern(dot(fs[code & 127], ft[lax.shift_right_logical(code, 7) & 31])))
@@ -317,6 +302,38 @@
     for j in range(AHEAD):
         tile(j, j)
 
+    def near_step(i):
+        for j in range(BUFS):
+            k = i * BUFS + j
+            multiply(k, j)
+            tile(k + AHEAD, (j + AHEAD) % BUFS)
+
+    def near_alone(i, carry):
+        near_step(i)
+        return carry
+
+    lax.fori_loop(0, ALONE, near_alone, 0)
+    climb_core()
+
+    for copy in bulk[:3]:
+        copy.wait()
+
+    def partner_points(l, carry):
+        at = lanes(l, LEAF)
+        source, target = features(ptp[:, at])
+        fs[LEAVES + l] = source.T.astype(bf16)
+        hi, lo = split(jnp.concatenate([dp[:, at], xp[:, at]], axis=0))
+        vt[LEAVES + l] = jnp.concatenate([hi, lo], axis=0)
+        return carry
+
+    lax.fori_loop(0, LEAVES, partner_points, 0, unroll=4)
+    late = [
+        pltpu.make_async_copy(a, b, late_sem.at[i])
+        for i, (a, b) in enumerate(((res_in, dp), (rhs_in, xp)))
+    ]
+    for load in late:
+        load.start()
+
     def near(i, carry):
         for r in range(3):
             @pl.when(i == RING_AT[r])
@@ -327,13 +344,10 @@
         def _():
             descend()
 
-        for j in range(BUFS):
-            k = i * BUFS + j
-            multiply(k, j)
-            tile(k + AHEAD, (j + AHEAD) % BUFS)
-        return carry
-
-    lax.fori_loop(0, STEPS, near, 0)
+        near_step(i)
+        return carry
+
+    lax.fori_loop(ALONE, STEPS, near, 0)
 
     for copy in bulk[3:]:
         copy.wait()
@@ -370,36 +384,41 @@
         return carry
 
     lax.fori_loop(0, LEAVES, turn, 0, unroll=8)
-    res_load.wait()
+    for load in late:
+        load.wait()
 
     def fold(value):
         return value[:, :128] + value[:, 128:]
 
+    def applied(l, at, rows):
+        bh, bl = split(lb[:, at])
+        zz = zt[l, rows]
+        pairs = terms[1 + l, rows] + terms[meta[ENDS + l], rows]
+        return pairs + (dot(zz, jnp.concatenate([bh, bh], axis=0)) + dot(zz[:, :64], bl))
+
     def finish(l, carry):
         at = lanes(l, LEAF)
-        bh, bl = split(lb[:, at])
-        zz = zt[l]
-        out = terms[meta[ENDS + l]] + (
-            dot(zz, jnp.concatenate([bh, bh], axis=0)) + dot(zz[:, :64], bl)
-        )
         dl = d[:, at]
         r = dp[:, at]
-        image = noise_level * dl + out[:COLS]
+        image = noise_level * dl + applied(l, at, pl.ds(0, COLS))
         tot[0] += fold(dl * image)
         tot[1] += fold(r * image)
         tot[2] += fold(image * image)
         tot[3] += fold(r * r)
         d[:, at] = image
-        x[:, at] = noise_level * x[:, at] + out[COLS:]
+        return carry
+
+    def finish_iterate(l, carry):
+        at = lanes(l, LEAF)
+        x[:, at] = xp[:, at] - (noise_level * x[:, at] + applied(l, at, pl.ds(COLS, COLS)))
         return carry
 
     lax.fori_loop(0, LEAVES, finish, 0, unroll=4)
     outs = [
         pltpu.make_async_copy(a, b, out_sem.at[i])
-        for i, (a, b) in enumerate(((d, hd_out), (x, hx_out)))
+        for i, (a, b) in enumerate(((d, hd_out), (x, gap_out)))
     ]
-    for out in outs:
-        out.start()
+    outs[0].start()
 
     lane = lax.broadcasted_iota(jnp.int32, (COLS, 128), 1)
     packed = zero
@@ -411,6 +430,9 @@
         copies = exchange(abuf, r, masks, asend, arecv)
         for copy in copies:
             copy.start()
+        if r == 1:
+            lax.fori_loop(0, LEAVES, finish_iterate, 0, unroll=4)
+            outs[1].start()
         for copy in copies:
             copy.wait()
         value = abuf[r, 0] + abuf[r, 1]
@@ -421,24 +443,36 @@
     new = old - 2.0 * alpha * cross + alpha * alpha * square
     beta = new / old
     eight = lax.broadcasted_iota(jnp.int32, (8, 128), 0)
-    scalars[...] = jnp.where(eight == 0, alpha, jnp.where(eight == 1, beta, 0.0))
+    value = jnp.where(eight == 0, alpha, jnp.where(eight == 1, beta, 0.0))
+    scalars[...] = jnp.concatenate([value, jnp.zeros((120, 128), f32)], axis=0).T[:COLS]
     for out in outs:
         out.wait()
 
 
 def lists(near_list, far_list):
-    counts = jnp.sum((near_list >= 0).astype(jnp.int32), axis=1)
+    others = jnp.sum((near_list >= 0).astype(jnp.int32), axis=1) - 1
     leaf = jnp.arange(LEAVES, dtype=jnp.int32)
-    before = jnp.sum(jnp.where(leaf[:, None] > leaf[None, :], counts[None, :], 0), axis=1)
-    place = before[:, None] + jnp.arange(8, dtype=jnp.int32)[None, :]
-    first = jnp.arange(8, dtype=jnp.int32)[None, :] == 0
-    code = near_list + leaf[:, None] * 128 + jnp.where(first, 0, 4096)
+    before = jnp.sum(jnp.where(leaf[:, None] > leaf[None, :], others[None, :], 0), axis=1) + LEAVES
+    slot8 = jnp.arange(8, dtype=jnp.int32)[None, :]
+    place = jnp.where(slot8 == 0, leaf[:, None], before[:, None] + slot8 - 1)
+    code = near_list + leaf[:, None] * 128 + jnp.where(slot8 < 2, 0, 4096)
     nothing = 64 + 31 * 128 + 4096
     slot = jnp.arange(SLOTS, dtype=jnp.int32)[:, None, None]
     hit = (place[None] == slot) & (near_list >= 0)[None]
     pairs = jnp.sum(jnp.where(hit, code[None] - nothing, 0), axis=(1, 2)) + nothing
+    ends = jnp.where(others > 0, before + others, 0)
     far = jnp.where(far_list < 0, 64, far_list).reshape(-1)
-    return jnp.concatenate([pairs, before + counts, far])
+    return jnp.concatenate([pairs, ends, far])
+
+
+def update_kernel(scalars, it, d, r, hd, gap, new_it, new_r, new_d, true_r):
+    alpha, beta = scalars[:, 0:1], scalars[:, 1:2]
+    dd, step = d[...], alpha * hd[...]
+    rr = r[...] - step
+    new_it[...] = it[...] + alpha * dd
+    new_r[...] = rr
+    new_d[...] = rr + beta * dd
+    true_r[...] = gap[...] - step
 
 
 def shards(
@@ -454,10 +488,10 @@
     point_buf = pltpu.VMEM(points.shape, f32)
     skel_buf = pltpu.VMEM(skeletons.shape, f32)
     dma = pltpu.SemaphoreType.DMA
-    hd, hx, scalars = pl.pallas_call(
+    hd, gap, scalars = pl.pallas_call(
         step_kernel,
-        out_shape=(wide, wide, jax.ShapeDtypeStruct((8, 128), f32)),
-        in_specs=[sm] + [hbm] * 9,
+        out_shape=(wide, wide, jax.ShapeDtypeStruct((COLS, 128), f32)),
+        in_specs=[sm] + [hbm] * 10,
         out_specs=(hbm, hbm, vm),
         scratch_shapes=[
             big, big, big,
@@ -485,22 +519,24 @@
             pltpu.VMEM((4, 64, 128), f32),
             pltpu.VMEM((4, 4, 8, 128), f32),
             dma((5 + 3 * CHUNKS,)), dma((6,)), dma((5,)), dma((5,)),
-            dma((4, 3)), dma((4, 3)), dma((4, 3)), dma((4, 3)), dma((2,)),
+            dma((4, 3)), dma((4, 3)), dma((4, 3)), dma((4, 3)), dma((2,)), dma((2,)),
         ],
         compiler_params=pltpu.CompilerParams(
             collective_id=0, has_side_effects=True, vmem_limit_bytes=VMEM_LIMIT
         ),
     )(
         lists(near_list, far_list), direction, iterate, leaf_basis, device_basis, transfer,
-        node_coords, points, skeletons, residual,
+        node_coords, points, skeletons, residual, rhs,
     )
-    alpha = scalars[0, :COLS][:, None]
-    beta = scalars[1, :COLS][:, None]
-    new_iterate = iterate + alpha * direction
-    new_residual = residual - alpha * hd
-    new_direction = new_residual + beta * direction
-    true_residual = rhs - (hx + alpha * hd)
-    return (new_iterate, new_residual, new_direction, true_residual)
+    block = pl.BlockSpec((COLS, UPDATE), lambda i: (0, i))
+    return pl.pallas_call(
+        update_kernel,
+        grid=(LEAVES * LEAF // UPDATE,),
+        out_shape=(wide,) * 4,
+        in_specs=[pl.BlockSpec((COLS, 128), lambda i: (0, 0))] + [block] * 5,
+        out_specs=(block,) * 4,
+        compiler_params=pltpu.CompilerParams(vmem_limit_bytes=VMEM_LIMIT),
+    )(scalars, iterate, direction, residual, hd, gap)
 
 
 def solution(mesh):

time: 85 us -> 79.2 us (0.932)
  other arithmetic: 11.1 us -> 2.51 us
  Pallas kernels: 71.9 us -> 75.5 us
    add x3 -> x1, other arithmetic: 8.72 us -> 0.01 us  [lists(): jnp.sum(jnp.where(leaf[:, None] > leaf[None, :], others[None, :], 0), axi...]
    pallas_call x0 -> x1, Pallas kernels: none -> 8 us  [shards(): pl.pallas_call(update_kernel, grid=(LEAVES * LEAF // UPDATE,), out_shape=...]
    pallas_call x1, Pallas kernels: 71.9 us -> 67.5 us  [shards(): pl.pallas_call(step_kernel, out_shape=(wide, wide, jax.ShapeDtypeStruct((...]
where the time goes in v3:
time: 79.2 us; the launch traced here: 79 us
  Pallas kernels  75.5 us (95%)
  other arithmetic  2.51 us (3%)
    pallas_call x1, Pallas kernels, shards(): pl.pallas_call(step_kernel, out_shape=(wide, wide, jax.ShapeDtypeStruct((...  67.5 us
    pallas_call x1, Pallas kernels, shards(): pl.pallas_call(update_kernel, grid=(LEAVES * LEAF // UPDATE,), out_shape=...  8 us

profile of v3, /device:TPU:0, one launch (start us, length us, event | category | flops | bytes accessed | tf_op | source)
XLA Modules:
  0.0 79.0 jit_solution(1727757253343417251)
XLA Ops:
  0.7 0.7 compare_select_fusion
  1.4 0.8 convert_reduce_fusion
  2.1 0.1 select_reduce_fusion.1
  2.2 0.1 copy.21
  2.3 0.1 copy.23
  2.4 0.1 reshape.77
  2.5 0.1 add_select_fusion
  2.6 0.1 copy.22
  2.7 0.2 select_reduce_fusion
  2.9 0.7 pad_add_fusion.meta
  3.5 67.5 %shard_map.147 = (f32[64,8192]{1,0:T(8,128)}, f32[64,8192]{1,0:T(8,128)}, f32[64,128]{1,0:T(8,128)}) custom-call(s32[488]{0:T(512)} %pad_add_fusion.meta, f32[64,8192]{1,0:T(8,128)} %d.1, f32[64,8192]{1,0:T(8,128)} %it.1, f32[64,8192]{1,0:T(8,128)} %lb_in.1, f32[64,2048]{1,0:T(8,128)} %db_in.1, f32[126,64,128]{2,1,0:T(8,128)} %transfer.1, f32[8,8064]{1,0:T(8,128)} %nc_in.1, ...), custom_call_target="tpu_custom_call" | custom-call | tf_op jit(solution)/shard_map/pallas_call | solution.py:491
  71.0 8.0 %shard_map.148 = (f32[64,8192]{1,0:T(8,128)}, f32[64,8192]{1,0:T(8,128)}, f32[64,8192]{1,0:T(8,128)}, f32[64,8192]{1,0:T(8,128)}) custom-call(f32[64,128]{1,0:T(8,128)} %get-tuple-element.7.scalars, f32[64,8192]{1,0:T(8,128)} %it.1, f32[64,8192]{1,0:T(8,128)} %d.1, f32[64,8192]{1,0:T(8,128)} %r.1, f32[64,8192]{1,0:T(8,128)} %get-tuple-element.8.hd, ...), custom_call_target="tpu_custom_call" | custom-call | tf_op jit(solution)/shard_map/pallas_call | solution.py:532
  (6 shorter events, 0.0 us)

commit v4 on v3

--- a/solution.py
+++ b/solution.py
@@ -17,13 +17,13 @@
 COORD = math.sqrt(3.0) / length_scale / LN2
 LEAVES, LEAF, RANK, COLS = 32, 256, 64, 64
 SLOTS, BUFS, AHEAD = 200, 8, 4
-ENDS, FARS = SLOTS, SLOTS + LEAVES
 STEPS, CHUNKS = 24, 4
 RING_AT, DOWN_AT = (5, 9, 13), 17
-ALONE, UPDATE = 3, 2048
+ALONE, UPDATE = 3, 16
 VMEM_LIMIT = 63 << 20
 CORE = (1,)
 RINGS = ((2, 4, 6), (8, 16, 24), (32, 64, 96))
+SUM_ROUNDS = (tuple(range(1, 8)), tuple(range(8, 128, 8)))
 
 
 def dot(a, b):
@@ -108,16 +108,57 @@
     ]
 
 
+def lists(near_in, far_in, flat_v, pairs_v, rows_v, pairs, rows_s, sems):
+    shape = (LEAVES, 256)
+    leaf = lax.broadcasted_iota(jnp.int32, shape, 0)
+    slot = lax.broadcasted_iota(jnp.int32, shape, 1)
+    tall = []
+    for i, ref in enumerate((near_in, far_in)):
+        flat_v[i] = jnp.full((8, 128), -1, jnp.int32)
+        flat_v[i, :, :LEAVES] = ref[...]
+        tall.append(flat_v[i].T[:LEAVES])
+    near, far = tall
+    entry = [jnp.broadcast_to(near[:, j : j + 1], shape) for j in range(8)]
+    others = jnp.zeros(shape, jnp.int32)
+    for j in range(1, 8):
+        others = others + jnp.where(entry[j] >= 0, 1, 0)
+    upto = others
+    for step in (1, 2, 4, 8, 16):
+        upto = upto + jnp.where(leaf >= step, pltpu.roll(upto, step, 0), 0)
+    before = upto - others + LEAVES
+    nothing = 64 + 31 * 128 + 4096
+    total = jnp.zeros(shape, jnp.int32)
+    for j in range(8):
+        place = leaf if j == 0 else before + (j - 1)
+        code = entry[j] + leaf * 128 + ((0 if j < 2 else 4096) - nothing)
+        total = total + jnp.where((place == slot) & (entry[j] >= 0), code, 0)
+    for step in (16, 8, 4, 2, 1):
+        total = total + pltpu.roll(total, step, 0)
+    pairs_v[...] = total[:8] + nothing
+    ends = jnp.where(others > 0, jnp.minimum(before + others, STEPS * BUFS), 0)
+    rows_v[...] = ends[:, :128]
+    rows_v[:, :8] = jnp.where(far < 0, 64, far)
+    copies = [
+        pltpu.make_async_copy(pairs_v, pairs, sems.at[0]),
+        pltpu.make_async_copy(rows_v, rows_s, sems.at[1]),
+    ]
+    for copy in copies:
+        copy.start()
+    return copies
+
+
 def step_kernel(
-    meta, d_in, x_in, lb_in, db_in, transfer, nc_in, pts_in, sk_in, res_in, rhs_in,
+    near_in, far_in, d_in, x_in, lb_in, db_in, transfer, nc_in, pts_in, sk_in, res_in, rhs_in,
     hd_out, gap_out, scalars,
     d, x, lb, db, nc, pts, sk, dp, xp, ptp, skp, w_own, wp,
     mats, kmask, buf, stk, z0, vt, fs, ft, wt, fte, fto, fsk, zl, zt, terms, kh, kl, tot, abuf,
     in_sem, mat_sem, far_send, far_recv, send, recv, asend, arecv, out_sem, late_sem,
+    flat_v, pairs_v, rows_v, pairs, rows_s, list_sem,
 ):
     q = tree_position()
-    every = CORE + sum(RINGS, ())
+    every = sum(SUM_ROUNDS, ())
     greet(every)
+    list_copies = lists(near_in, far_in, flat_v, pairs_v, rows_v, pairs, rows_s, list_sem)
     chunk = LEAVES * LEAF // CHUNKS
     loads = [
         pltpu.make_async_copy(a, b, in_sem.at[i])
@@ -285,13 +326,13 @@
         z0[...] = down
 
     def tile(k, b):
-        code = meta[k]
+        code = pairs[0, k]
         hi, lo = split(kern(dot(fs[code & 127], ft[lax.shift_right_logical(code, 7) & 31])))
         kh[b] = hi
         kl[b] = lo
 
     def multiply(k, b):
-        code = meta[k]
+        code = pairs[0, k]
         v = vt[code & 127]
         keep = lax.shift_right_logical(code, 12).astype(f32)
         both = dot(v, kh[b])
@@ -299,6 +340,8 @@
             both[: 2 * COLS] + both[2 * COLS :] + dot(v[: 2 * COLS], kl[b])
         )
 
+    for copy in list_copies:
+        copy.wait()
     for j in range(AHEAD):
         tile(j, j)
 
@@ -367,7 +410,7 @@
         across = []
         rows = []
         for j in range(4):
-            one, two = meta[FARS + l * 8 + 2 * j], meta[FARS + l * 8 + 2 * j + 1]
+            one, two = rows_s[l, 2 * j], rows_s[l, 2 * j + 1]
             across.append(fte[one] + fto[two])
             rows += [wt[one], wt[two]]
         hi, lo = split(kern(dot(fsk[l], jnp.concatenate(across, axis=1))))
@@ -393,7 +436,7 @@
     def applied(l, at, rows):
         bh, bl = split(lb[:, at])
         zz = zt[l, rows]
-        pairs = terms[1 + l, rows] + terms[meta[ENDS + l], rows]
+        pairs = terms[1 + l, rows] + terms[rows_s[l, 8], rows]
         return pairs + (dot(zz, jnp.concatenate([bh, bh], axis=0)) + dot(zz[:, :64], bl))
 
     def finish(l, carry):
@@ -425,19 +468,17 @@
     for i in range(4):
         packed = jnp.where(lane == i, jnp.sum(tot[i], axis=1, keepdims=True), packed)
     value = jnp.concatenate([packed, zero], axis=0).T[:8]
-    for r, masks in enumerate((CORE,) + RINGS):
+    for r, masks in enumerate(SUM_ROUNDS):
         abuf[r, 0] = value
         copies = exchange(abuf, r, masks, asend, arecv)
         for copy in copies:
             copy.start()
-        if r == 1:
+        if r == 0:
             lax.fori_loop(0, LEAVES, finish_iterate, 0, unroll=4)
             outs[1].start()
         for copy in copies:
             copy.wait()
-        value = abuf[r, 0] + abuf[r, 1]
-        if len(masks) == 3:
-            value = value + (abuf[r, 2] + abuf[r, 3])
+        value = jnp.sum(abuf[r, : len(masks) + 1], axis=0)
     curv, cross, square, old = value[0:1], value[1:2], value[2:3], value[3:4]
     alpha = old / curv
     new = old - 2.0 * alpha * cross + alpha * alpha * square
@@ -449,22 +490,6 @@
         out.wait()
 
 
-def lists(near_list, far_list):
-    others = jnp.sum((near_list >= 0).astype(jnp.int32), axis=1) - 1
-    leaf = jnp.arange(LEAVES, dtype=jnp.int32)
-    before = jnp.sum(jnp.where(leaf[:, None] > leaf[None, :], others[None, :], 0), axis=1) + LEAVES
-    slot8 = jnp.arange(8, dtype=jnp.int32)[None, :]
-    place = jnp.where(slot8 == 0, leaf[:, None], before[:, None] + slot8 - 1)
-    code = near_list + leaf[:, None] * 128 + jnp.where(slot8 < 2, 0, 4096)
-    nothing = 64 + 31 * 128 + 4096
-    slot = jnp.arange(SLOTS, dtype=jnp.int32)[:, None, None]
-    hit = (place[None] == slot) & (near_list >= 0)[None]
-    pairs = jnp.sum(jnp.where(hit, code[None] - nothing, 0), axis=(1, 2)) + nothing
-    ends = jnp.where(others > 0, before + others, 0)
-    far = jnp.where(far_list < 0, 64, far_list).reshape(-1)
-    return jnp.concatenate([pairs, ends, far])
-
-
 def update_kernel(scalars, it, d, r, hd, gap, new_it, new_r, new_d, true_r):
     alpha, beta = scalars[:, 0:1], scalars[:, 1:2]
     dd, step = d[...], alpha * hd[...]
@@ -480,7 +505,6 @@
     node_coords, near_list, far_list,
 ):
     vm = pl.BlockSpec(memory_space=pltpu.VMEM)
-    sm = pl.BlockSpec(memory_space=pltpu.SMEM)
     hbm = pl.BlockSpec(memory_space=pl.ANY)
     wide = jax.ShapeDtypeStruct((COLS, LEAVES * LEAF), f32)
     big = pltpu.VMEM((COLS, LEAVES * LEAF), f32)
@@ -491,7 +515,7 @@
     hd, gap, scalars = pl.pallas_call(
         step_kernel,
         out_shape=(wide, wide, jax.ShapeDtypeStruct((COLS, 128), f32)),
-        in_specs=[sm] + [hbm] * 10,
+        in_specs=[vm] * 2 + [hbm] * 10,
         out_specs=(hbm, hbm, vm),
         scratch_shapes=[
             big, big, big,
@@ -517,23 +541,29 @@
             pltpu.VMEM((BUFS, 256, 256), bf16),
             pltpu.VMEM((BUFS, 256, 256), bf16),
             pltpu.VMEM((4, 64, 128), f32),
-            pltpu.VMEM((4, 4, 8, 128), f32),
+            pltpu.VMEM((2, 16, 8, 128), f32),
             dma((5 + 3 * CHUNKS,)), dma((6,)), dma((5,)), dma((5,)),
-            dma((4, 3)), dma((4, 3)), dma((4, 3)), dma((4, 3)), dma((2,)), dma((2,)),
+            dma((4, 3)), dma((4, 3)), dma((2, 15)), dma((2, 15)), dma((2,)), dma((2,)),
+            pltpu.VMEM((2, 8, 128), jnp.int32),
+            pltpu.VMEM((8, 256), jnp.int32),
+            pltpu.VMEM((LEAVES, 128), jnp.int32),
+            pltpu.SMEM((8, 256), jnp.int32),
+            pltpu.SMEM((LEAVES, 128), jnp.int32),
+            dma((2,)),
         ],
         compiler_params=pltpu.CompilerParams(
             collective_id=0, has_side_effects=True, vmem_limit_bytes=VMEM_LIMIT
         ),
     )(
-        lists(near_list, far_list), direction, iterate, leaf_basis, device_basis, transfer,
+        near_list.T, far_list.T, direction, iterate, leaf_basis, device_basis, transfer,
         node_coords, points, skeletons, residual, rhs,
     )
-    block = pl.BlockSpec((COLS, UPDATE), lambda i: (0, i))
+    block = pl.BlockSpec((UPDATE, LEAVES * LEAF), lambda i: (i, 0))
     return pl.pallas_call(
         update_kernel,
-        grid=(LEAVES * LEAF // UPDATE,),
+        grid=(COLS // UPDATE,),
         out_shape=(wide,) * 4,
-        in_specs=[pl.BlockSpec((COLS, 128), lambda i: (0, 0))] + [block] * 5,
+        in_specs=[pl.BlockSpec((UPDATE, 128), lambda i: (i, 0))] + [block] * 5,
         out_specs=(block,) * 4,
         compiler_params=pltpu.CompilerParams(vmem_limit_bytes=VMEM_LIMIT),
     )(scalars, iterate, direction, residual, hd, gap)

time: 79.2 us -> 73.6 us (0.929)
  Pallas kernels: 75.5 us -> 72.7 us
  other arithmetic: 2.51 us -> 0 us
    pallas_call x1, Pallas kernels: 67.5 us -> 65.2 us  [shards(): pl.pallas_call(step_kernel, out_shape=(wide, wide, jax.ShapeDtypeStruct((...]
    reduce_sum x3 -> x0, other arithmetic: 1.06 us -> none  [the longest x1 0.76 us: lists(): others = jnp.sum((near_list >= 0).astype(jnp.int32), axis=1) - 1]
where the time goes in v4:
time: 73.6 us; the launch traced here: 73.3 us
  Pallas kernels  72.7 us (99%)
    pallas_call x1, Pallas kernels, shards(): pl.pallas_call(step_kernel, out_shape=(wide, wide, jax.ShapeDtypeStruct((...  65.2 us
    pallas_call x1, Pallas kernels, shards(): pl.pallas_call(update_kernel, grid=(COLS // UPDATE,), out_shape=(wide,) *...  7.42 us

profile of v4, /device:TPU:0, one launch (start us, length us, event | category | flops | bytes accessed | tf_op | source)
XLA Modules:
  0.0 73.3 jit_solution(16702296637989513646)
XLA Ops:
  0.6 65.2 %shard_map.147 = (f32[64,8192]{1,0:T(8,128)}, f32[64,8192]{1,0:T(8,128)}, f32[64,128]{1,0:T(8,128)}) custom-call(s32[8,32]{1,0:T(8,128)} %bitcast.2, s32[8,32]{1,0:T(8,128)} %bitcast.3, f32[64,8192]{1,0:T(8,128)} %d.1, f32[64,8192]{1,0:T(8,128)} %it.1, f32[64,8192]{1,0:T(8,128)} %lb_in.1, f32[64,2048]{1,0:T(8,128)} %db_in.1, f32[126,64,128]{2,1,0:T(8,128)} %transfer.1, ...), custom_call_target="tpu_custom_call" | custom-call | tf_op jit(solution)/shard_map/pallas_call | solution.py:515
  65.9 7.4 %shard_map.148 = (f32[64,8192]{1,0:T(8,128)}, f32[64,8192]{1,0:T(8,128)}, f32[64,8192]{1,0:T(8,128)}, f32[64,8192]{1,0:T(8,128)}) custom-call(f32[64,128]{1,0:T(8,128)} %get-tuple-element.7.scalars, f32[64,8192]{1,0:T(8,128)} %it.1, f32[64,8192]{1,0:T(8,128)} %d.1, f32[64,8192]{1,0:T(8,128)} %r.1, f32[64,8192]{1,0:T(8,128)} %get-tuple-element.8.hd, ...), custom_call_target="tpu_custom_call" | custom-call | tf_op jit(solution)/shard_map/pallas_call | solution.py:562
